TPU v7x, 32 devices: a whole 2x2x4 slice. The times are simulated.
32 devices in a mesh: groups: 2 (over y), img: 4 (over z), cap: 4 (over x, core).
Axes of the slice: x: 2, y: 2, z: 4, core: 2. Of those that a mesh axis runs over, the one named last changes fastest.
Arguments:
- text_states: bfloat16 [512, 32, 768], P(('groups', 'img', 'cap')), parts along dimension 0, may hold values from -170 to 170
- text_lens: int32 [512], P(('groups', 'img', 'cap')), parts along dimension 0, may hold values from 8 to 32
- text_proj: bfloat16 [768, 256], replicated, may hold values from -1.75 to 1.75
- query_states: bfloat16 [192, 32, 768], P(('groups', 'img')), parts along dimension 0, may hold values from -170 to 170
- vision_proj: bfloat16 [768, 256], replicated, may hold values from -1.75 to 1.75
- student_text: bfloat16 [512, 512], P(('groups', 'img', 'cap')), parts along dimension 0, may hold values from -6 to 6
- student_feats: bfloat16 [192, 768], P(('groups', 'img')), parts along dimension 0, may hold values from -170 to 170
- student_proj: bfloat16 [768, 512], replicated, may hold values from -1.75 to 1.75
- candidates: int32 [512, 64], P(('groups', 'img', 'cap')), parts along dimension 0, may hold values from 0 to 95, as said below
Outputs:
- losses: float32 [512], P(('groups', 'img', 'cap')), parts along dimension 0
- proj_grad: float32 [1536, 512], P('groups'), parts along dimension 0
There are 2 independent parts, one for each index of `groups`. A program takes and returns all parts, laid end to end along the dimension named above; an argument that names none is the same for every part. Nothing has to cross between parts.
Inputs may be any that keep to these rules, and one draw needn't show every extreme that they name: Each row of candidates is 8 blocks of 8 consecutive entries; the ids of one block are distinct and all belong to one index of img (id // 24). The blocks of the 16 captions of one device name one index of img at most 64 times, and exactly 64 times for some index.
All inputs are finite; a program needn't handle non-finite values.
Results may differ from a plain program's by a relative error of at most 0.004.
Values may be sent and summed in bfloat16 or wider, within the bound.
A program may use at most 64 MiB of HBM per device.

v0:
```python
import jax
import jax.numpy as jnp
from jax import lax
from jax.sharding import PartitionSpec as P

BLOCK = 8


TEACHER_TEMP = 0.01
LOGIT_SCALE = 100.0


def unit_rows(values):
    return values * lax.rsqrt(jnp.sum(values * values, axis=-1, keepdims=True) + 1e-06)


def pooled_scores(token_rows, lengths, query_rows, image_count):
    row_count, length, feature_width = token_rows.shape
    products = jnp.einsum(
        "rt,jt->rj",
        token_rows.reshape(-1, feature_width),
        query_rows,
        preferred_element_type=jnp.float32,
    )
    strongest = jnp.max(products.reshape(row_count, length, image_count, -1), axis=-1)
    valid_mask = jnp.arange(length)[None, :] < lengths[:, None]
    summed = jnp.sum(jnp.where(valid_mask[:, :, None], strongest, 0.0), axis=1)
    return summed / jnp.maximum(lengths, 1)[:, None].astype(jnp.float32) / TEACHER_TEMP


def listwise(teacher, student):
    teacher_log = jax.nn.log_softmax(teacher, axis=-1)
    student_log = jax.nn.log_softmax(student, axis=-1)
    teacher_prob = jnp.exp(teacher_log)
    losses = jnp.sum(teacher_prob * (teacher_log - student_log), axis=-1)
    return (losses, jnp.exp(student_log) - teacher_prob)


def split_parts(values):
    top_part = lax.optimization_barrier(values.astype(jnp.bfloat16))
    rest_part = (values - top_part.astype(jnp.float32)).astype(jnp.bfloat16)
    return (top_part, rest_part)


def feature_product(features, top_part, rest_part):
    leading = jnp.einsum("is,id->sd", features, top_part, preferred_element_type=jnp.float32)
    return leading + jnp.einsum(
        "is,id->sd", features, rest_part, preferred_element_type=jnp.float32
    )


def local(
    text_states,
    text_lens,
    text_proj,
    query_states,
    vision_proj,
    student_text,
    student_feats,
    student_proj,
    candidates,
):
    cap_dev, length, txt_width = text_states.shape
    img_dev, query_count = (query_states.shape[0], query_states.shape[1])
    cand_count = candidates.shape[1]
    itc_width = text_proj.shape[1]
    embed_width = student_proj.shape[1]
    token_rows = (
        unit_rows(
            jnp.dot(
                text_states.reshape(-1, txt_width), text_proj, preferred_element_type=jnp.float32
            )
        )
        .astype(jnp.bfloat16)
        .reshape(cap_dev, length, itc_width)
    )
    query_rows = unit_rows(
        jnp.dot(
            query_states.reshape(-1, txt_width), vision_proj, preferred_element_type=jnp.float32
        )
    ).astype(jnp.bfloat16)
    image_embed = jnp.dot(student_feats, student_proj, preferred_element_type=jnp.float32)
    image_norm = jnp.sqrt(jnp.sum(image_embed * image_embed, axis=-1) + 1e-06)
    image_unit = image_embed / image_norm[:, None]
    img_count = lax.axis_size("img")
    per_list = cand_count // BLOCK
    block_count = cap_dev * per_list
    slot_count = max(2, 2 * block_count // img_count)
    slot_total = img_count * slot_count
    block_ids = candidates.reshape(block_count, BLOCK)
    owners = block_ids[:, 0] // img_dev
    owner_hits = (owners[:, None] == jnp.arange(img_count)[None, :]).astype(jnp.int32)
    earlier = jnp.cumsum(owner_hits, axis=0) - owner_hits
    target = owners * slot_count + jnp.sum(earlier * owner_hits, axis=1)
    source = (
        jnp.full((slot_total,), block_count, jnp.int32)
        .at[target]
        .set(jnp.arange(block_count, dtype=jnp.int32))
    )
    filled = source < block_count
    source_block = jnp.minimum(source, block_count - 1)
    source_caption = source_block // per_list
    send_tokens = jnp.where(
        filled[:, None, None], token_rows[source_caption], jnp.zeros((), jnp.bfloat16)
    )
    send_text = jnp.where(
        filled[:, None], student_text[source_caption], jnp.zeros((), jnp.bfloat16)
    )
    send_meta = jnp.where(
        filled[:, None],
        jnp.concatenate(
            [block_ids[source_block] % img_dev, text_lens[source_caption][:, None]], axis=1
        ),
        0,
    ).astype(jnp.bfloat16)
    recv_tokens, recv_text, recv_meta = (
        lax.all_to_all(
            send_tokens.reshape(img_count, slot_count, length, itc_width),
            "img",
            split_axis=0,
            concat_axis=0,
            tiled=True,
        ),
        lax.all_to_all(
            send_text.reshape(img_count, slot_count, embed_width),
            "img",
            split_axis=0,
            concat_axis=0,
            tiled=True,
        ),
        lax.all_to_all(
            send_meta.reshape(img_count, slot_count, BLOCK + 1),
            "img",
            split_axis=0,
            concat_axis=0,
            tiled=True,
        ),
    )
    recv_tokens = recv_tokens.reshape(slot_total, length, itc_width)
    recv_meta = recv_meta.reshape(slot_total, BLOCK + 1).astype(jnp.int32)
    local_ids = recv_meta[:, :BLOCK]
    recv_lens = recv_meta[:, BLOCK]
    group_slots = min(slot_total, max(1, 2048 // length))
    group_count = slot_total // group_slots

    def score_slots(inputs):
        return pooled_scores(inputs[0], inputs[1], query_rows, img_dev)

    pooled = lax.map(
        score_slots,
        (
            recv_tokens.reshape(group_count, group_slots, length, itc_width),
            recv_lens.reshape(group_count, group_slots),
        ),
    ).reshape(slot_total, img_dev)
    selector = (local_ids[:, :, None] == jnp.arange(img_dev)[None, None, :]).astype(jnp.float32)
    teacher_rows = jnp.sum(selector * pooled[:, None, :], axis=-1)
    text_unit = unit_rows(recv_text.reshape(slot_total, embed_width).astype(jnp.float32))
    cosine = jnp.dot(text_unit, image_unit.T, precision=lax.Precision.HIGHEST)
    student_rows = LOGIT_SCALE * jnp.sum(selector * cosine[:, None, :], axis=-1)
    back_teacher, back_student = (
        lax.all_to_all(
            teacher_rows.reshape(img_count, slot_count, BLOCK),
            "img",
            split_axis=0,
            concat_axis=0,
            tiled=True,
        ),
        lax.all_to_all(
            student_rows.reshape(img_count, slot_count, BLOCK),
            "img",
            split_axis=0,
            concat_axis=0,
            tiled=True,
        ),
    )
    teacher = back_teacher.reshape(slot_total, BLOCK)[target].reshape(cap_dev, cand_count)
    student = back_student.reshape(slot_total, BLOCK)[target].reshape(cap_dev, cand_count)
    losses, score_grad = listwise(teacher, student)
    send_grad = jnp.where(
        filled[:, None], score_grad.reshape(block_count, BLOCK)[source_block], 0.0
    )
    recv_grad = lax.all_to_all(
        send_grad.reshape(img_count, slot_count, BLOCK),
        "img",
        split_axis=0,
        concat_axis=0,
        tiled=True,
    ).reshape(slot_total, BLOCK)
    spread = jnp.sum(selector * (LOGIT_SCALE * recv_grad)[:, :, None], axis=1)
    radial = jnp.sum(spread * cosine, axis=0)
    embed_grad = (
        jnp.einsum("si,sd->id", spread, text_unit, precision=lax.Precision.HIGHEST)
        - radial[:, None] * image_unit
    ) / image_norm[:, None]
    top_part, rest_part = split_parts(embed_grad)
    proj_grad = lax.psum(feature_product(student_feats, top_part, rest_part), ("img", "cap"))
    return (losses, proj_grad)


def solution(mesh):
    in_specs = (
        P(("groups", "img", "cap"), None, None),
        P(("groups", "img", "cap")),
        P(),
        P(("groups", "img"), None, None),
        P(),
        P(("groups", "img", "cap"), None),
        P(("groups", "img"), None),
        P(),
        P(("groups", "img", "cap"), None),
    )
    out_specs = (P(("groups", "img", "cap")), P("groups", None))
    return jax.shard_map(local, mesh=mesh, in_specs=in_specs, out_specs=out_specs, check_vma=False)
```

profile of v0, /device:TPU:0, one launch (start us, length us, event | category | flops | bytes accessed | tf_op | source)
XLA Modules:
  0.0 322.4 jit_solution(15707511335517866304)
XLA Ops:
  7.2 1.9 fusion.16
  9.2 0.8 reshape.188
  10.8 1.0 scatter_custom_fusion
  11.9 10.0 %compare_select_fusion.1 = (s32[256]{0:T(256)S(1)}, s32[256]{0:T(256)S(1)}, s32[256]{0:T(256)S(1)}) fusion(s32[256]{0:T(256)S(1)} %scatter_custom_fusion, s32[]{:T(128)} %bitcast.24, s32[]{:T(128)} %bitcast.23, s32[]{:T(128)} %bitcast.22, s32[]{:T(128)} %bitcast.21, s32[]{:T(128)} %bitcast.20, s32[]{:T(128)} %bitcast.19, s32[]{:T(128)} %bitcast.18, ...), kind=kLoop, calls=%fused_computation.65 | loop fusion | flops 13056 | bytes 4160 | tf_op jit(solution)/shard_map/select_n | solution.py:112
  21.8 0.7 gather_fusion
  23.5 6.3 %all-to-all-start = ((bf16[4,2,288]{2,1,0:T(2,128)(2,1)}), bf16[4,2,288]{2,1,0:T(2,128)(2,1)S(1)}, u32[]{:S(2)}, u32[]{:S(2)}) async-start(bf16[4,2,288]{2,1,0:T(2,128)(2,1)} %reshape.297), calls=%async_computation | async-start | bytes 12288 | tf_op jit(solution)/shard_map/all_to_all | solution.py:131
  30.5 1.2 gather_fusion.3
  31.6 0.8 broadcast_select_fusion.1
  32.4 2.7 gather_fusion.1
  35.4 4.8 %all-to-all-start.3 = ((bf16[4,64,512]{2,1,0:T(8,128)(2,1)}), bf16[4,64,512]{2,1,0:T(8,128)(2,1)S(1)}, u32[]{:S(2)}, u32[]{:S(2)}) async-start(bf16[4,64,512]{2,1,0:T(8,128)(2,1)} %broadcast_select_fusion.1), calls=%async_computation.3 | async-start | bytes 524288 | tf_op jit(solution)/shard_map/all_to_all | solution.py:124
  40.3 3.8 %broadcast_select_fusion = bf16[4,64,32,256]{3,2,1,0:T(8,128)(2,1)} fusion(bf16[4,64,32,256]{3,2,1,0:T(8,128)(2,1)} %bitcast.96, pred[4,64]{1,0:T(4,128)(4,1)S(1)} %broadcast_in_dim.72), kind=kLoop, calls=%fused_computation.19 | loop fusion | flops 2097152 | bytes 8388864 | tf_op jit(solution)/shard_map/jit(_where)/select_n | solution.py:103
  44.1 4.5 %all-to-all-done.3 = bf16[4,64,512]{2,1,0:T(8,128)(2,1)S(1)} async-done(((bf16[4,64,512]{2,1,0:T(8,128)(2,1)}), bf16[4,64,512]{2,1,0:T(8,128)(2,1)S(1)}, u32[]{:S(2)}, u32[]{:S(2)}) %all-to-all-start.3) | async-done | bytes 262176 | tf_op jit(solution)/shard_map/all_to_all | solution.py:124
  48.6 4.9 %all-to-all-start.1 = ((bf16[4,64,32,256]{3,2,1,0:T(8,128)(2,1)}), bf16[4,64,32,256]{3,2,1,0:T(8,128)(2,1)}, u32[]{:S(2)}, u32[]{:S(2)}) async-start(bf16[4,64,32,256]{3,2,1,0:T(8,128)(2,1)} %broadcast_select_fusion), calls=%async_computation.1 | async-start | bytes 8388608 | tf_op jit(solution)/shard_map/all_to_all | solution.py:117
  56.2 87.6 %all-to-all-done.1 = bf16[4,64,32,256]{3,2,1,0:T(8,128)(2,1)} async-done(((bf16[4,64,32,256]{3,2,1,0:T(8,128)(2,1)}), bf16[4,64,32,256]{3,2,1,0:T(8,128)(2,1)}, u32[]{:S(2)}, u32[]{:S(2)}) %all-to-all-start.1) | async-done | bytes 4194336 | tf_op jit(solution)/shard_map/all_to_all | solution.py:117
  143.8 41.4 %while.10 = (s32[]{:T(128)}, f32[4,64,24]{2,1,0:T(8,128)S(1)}, s32[4,64]{1,0:T(4,128)S(1)}, bf16[4,64,32,256]{3,2,1,0:T(8,128)(2,1)}, bf16[768,256]{1,0:T(8,128)(2,1)S(1)}, /*index=5*/s32[]{:T(128)}) while((s32[]{:T(128)}, f32[4,64,24]{2,1,0:T(8,128)S(1)}, s32[4,64]{1,0:T(4,128)S(1)}, bf16[4,64,32,256]{3,2,1,0:T(8,128)(2,1)}, ...), condition=%wide.region_8.9_spmd, body=%wide.region_5.8_spmd.sunk | while | flops 806932096 | bytes 1912909 | solution.py:149
  143.8 9.9 %convolution_reduce_fusion.2 = f32[64,32,24]{1,2,0:T(8,128)S(1)} fusion(bf16[24,32,256,1]{2,1,0,3:T(8,128)(2,1)S(1)} %bitcast.103, bf16[4,64,32,256]{3,2,1,0:T(8,128)(2,1)} %get-tuple-element.168, s32[]{:T(128)} %get-tuple-element.159), kind=kOutput, calls=%fused_computation.7.clone.1 | convolution fusion | flops 806830080 | bytes 1638912 | tf_op jit(solution)/shard_map/while/body/eval_jaxpr/rt,jt->rj/dot_general | solution.py:19
  154.1 9.9 %convolution_reduce_fusion.2 = f32[64,32,24]{1,2,0:T(8,128)S(1)} fusion(bf16[24,32,256,1]{2,1,0,3:T(8,128)(2,1)S(1)} %bitcast.103, bf16[4,64,32,256]{3,2,1,0:T(8,128)(2,1)} %get-tuple-element.168, s32[]{:T(128)} %get-tuple-element.159), kind=kOutput, calls=%fused_computation.7.clone.1 | convolution fusion | flops 806830080 | bytes 1638912 | tf_op jit(solution)/shard_map/while/body/eval_jaxpr/rt,jt->rj/dot_general | solution.py:19
  164.5 9.9 %convolution_reduce_fusion.2 = f32[64,32,24]{1,2,0:T(8,128)S(1)} fusion(bf16[24,32,256,1]{2,1,0,3:T(8,128)(2,1)S(1)} %bitcast.103, bf16[4,64,32,256]{3,2,1,0:T(8,128)(2,1)} %get-tuple-element.168, s32[]{:T(128)} %get-tuple-element.159), kind=kOutput, calls=%fused_computation.7.clone.1 | convolution fusion | flops 806830080 | bytes 1638912 | tf_op jit(solution)/shard_map/while/body/eval_jaxpr/rt,jt->rj/dot_general | solution.py:19
  174.9 9.9 %convolution_reduce_fusion.2 = f32[64,32,24]{1,2,0:T(8,128)S(1)} fusion(bf16[24,32,256,1]{2,1,0,3:T(8,128)(2,1)S(1)} %bitcast.103, bf16[4,64,32,256]{3,2,1,0:T(8,128)(2,1)} %get-tuple-element.168, s32[]{:T(128)} %get-tuple-element.159), kind=kOutput, calls=%fused_computation.7.clone.1 | convolution fusion | flops 806830080 | bytes 1638912 | tf_op jit(solution)/shard_map/while/body/eval_jaxpr/rt,jt->rj/dot_general | solution.py:19
  186.1 3.2 %all-to-all-start.2 = ((f32[4,1,512]{2,1,0:T(1,128)}), f32[4,1,512]{2,1,0:T(1,128)S(1)}, u32[]{:S(2)}, u32[]{:S(2)}) async-start(f32[4,1,512]{2,1,0:T(1,128)} %reshape.301), calls=%async_computation.2 | async-start | bytes 16384 | tf_op jit(solution)/shard_map/all_to_all | solution.py:162
  190.2 4.8 %all-to-all-done.2 = f32[4,1,512]{2,1,0:T(1,128)S(1)} async-done(((f32[4,1,512]{2,1,0:T(1,128)}), f32[4,1,512]{2,1,0:T(1,128)S(1)}, u32[]{:S(2)}, u32[]{:S(2)}) %all-to-all-start.2) | async-done | bytes 8224 | tf_op jit(solution)/shard_map/all_to_all | solution.py:162
  194.9 3.2 %all-to-all-start.4 = ((f32[4,1,512]{2,1,0:T(1,128)}), f32[4,1,512]{2,1,0:T(1,128)S(1)}, u32[]{:S(2)}, u32[]{:S(2)}) async-start(f32[4,1,512]{2,1,0:T(1,128)} %reshape.299), calls=%async_computation.4 | async-start | bytes 16384 | tf_op jit(solution)/shard_map/all_to_all | solution.py:169
  198.8 0.7 reduce.10
  200.8 3.0 all-to-all-done.4
  203.7 0.7 reduce.9
  205.7 0.7 exponential_subtract_fusion
  206.5 0.7 gather_fusion.5
  207.4 7.9 %all_to_all.30 = f32[4,1,512]{2,1,0:T(1,128)S(1)} all-to-all(f32[4,1,512]{2,1,0:T(1,128)S(1)} %reshape.303), channel_id=1, replica_groups=mesh['groups'=2,'img'=4,'cap'=4] {'img'}, dimensions={0} | all-to-all | bytes 16384 | tf_op jit(solution)/shard_map/all_to_all | solution.py:183
  215.3 0.7 reduce.11
  217.2 1.5 add_bitcast_fusion
  218.7 93.9 %all-reduce.2.cloned.1.call-done = f32[768,512]{0,1:T(8,128)} async-done(((f32[768,512]{0,1:T(8,128)}), f32[768,512]{0,1:T(8,128)}) %all-reduce.2.cloned.1.call-update) | async-done | bytes 1572880 | tf_op jit(solution)/shard_map/psum | solution.py:197
  312.6 3.0 copy.94
  (109 shorter events, 13.2 us)
Async XLA Ops:
  7.2 46.3 %copy-start = (bf16[24,32,768]{2,1,0:T(8,128)(2,1)S(1)}, bf16[24,32,768]{2,1,0:T(8,128)(2,1)}, u32[]{:S(2)}) copy-start(bf16[24,32,768]{2,1,0:T(8,128)(2,1)} %param.15) | copy-start | bytes 3538948
  7.2 22.7 %copy-start.3 = (bf16[16,32,768]{2,1,0:T(8,128)(2,1)S(1)}, bf16[16,32,768]{2,1,0:T(8,128)(2,1)}, u32[]{:S(2)}) copy-start(bf16[16,32,768]{2,1,0:T(8,128)(2,1)} %param.12) | copy-start | bytes 2359300
  7.2 22.7 %copy-start.5 = (bf16[768,256]{1,0:T(8,128)(2,1)S(1)}, bf16[768,256]{1,0:T(8,128)(2,1)}, u32[]{:S(2)}) copy-start(bf16[768,256]{1,0:T(8,128)(2,1)} %param.14) | copy-start | bytes 1179652
  21.8 8.6 %copy-start.1 = (bf16[16,512]{1,0:T(8,128)(2,1)S(1)}, bf16[16,512]{1,0:T(8,128)(2,1)}, u32[]{:S(2)}) copy-start(bf16[16,512]{1,0:T(8,128)(2,1)} %param.17) | copy-start | bytes 49156
  23.5 11.9 %all-to-all-start = ((bf16[4,2,288]{2,1,0:T(2,128)(2,1)}), bf16[4,2,288]{2,1,0:T(2,128)(2,1)S(1)}, u32[]{:S(2)}, u32[]{:S(2)}) async-start(bf16[4,2,288]{2,1,0:T(2,128)(2,1)} %reshape.297), calls=%async_computation | async-start | bytes 12288 | tf_op jit(solution)/shard_map/all_to_all | solution.py:131
  35.4 13.2 %all-to-all-start.3 = ((bf16[4,64,512]{2,1,0:T(8,128)(2,1)}), bf16[4,64,512]{2,1,0:T(8,128)(2,1)S(1)}, u32[]{:S(2)}, u32[]{:S(2)}) async-start(bf16[4,64,512]{2,1,0:T(8,128)(2,1)} %broadcast_select_fusion.1), calls=%async_computation.3 | async-start | bytes 524288 | tf_op jit(solution)/shard_map/all_to_all | solution.py:124
  44.1 9.4 %copy-start.4 = (bf16[768,256]{1,0:T(8,128)(2,1)S(1)}, bf16[768,256]{1,0:T(8,128)(2,1)}, u32[]{:S(2)}) copy-start(bf16[768,256]{1,0:T(8,128)(2,1)} %param.16) | copy-start | bytes 1179652
  48.6 95.2 %all-to-all-start.1 = ((bf16[4,64,32,256]{3,2,1,0:T(8,128)(2,1)}), bf16[4,64,32,256]{3,2,1,0:T(8,128)(2,1)}, u32[]{:S(2)}, u32[]{:S(2)}) async-start(bf16[4,64,32,256]{3,2,1,0:T(8,128)(2,1)} %broadcast_select_fusion), calls=%async_computation.1 | async-start | bytes 8388608 | tf_op jit(solution)/shard_map/all_to_all | solution.py:117
  53.5 1.1 copy-start.2
  53.5 1.1 copy-start.6
  186.1 8.8 %all-to-all-start.2 = ((f32[4,1,512]{2,1,0:T(1,128)}), f32[4,1,512]{2,1,0:T(1,128)S(1)}, u32[]{:S(2)}, u32[]{:S(2)}) async-start(f32[4,1,512]{2,1,0:T(1,128)} %reshape.301), calls=%async_computation.2 | async-start | bytes 16384 | tf_op jit(solution)/shard_map/all_to_all | solution.py:162
  194.9 8.8 %all-to-all-start.4 = ((f32[4,1,512]{2,1,0:T(1,128)}), f32[4,1,512]{2,1,0:T(1,128)S(1)}, u32[]{:S(2)}, u32[]{:S(2)}) async-start(f32[4,1,512]{2,1,0:T(1,128)} %reshape.299), calls=%async_computation.4 | async-start | bytes 16384 | tf_op jit(solution)/shard_map/all_to_all | solution.py:169
  198.2 114.4 %all-reduce.2.cloned.1.call-start = ((), (), s32[]{:S(2)}) async-start(), calls=%async_computation.6 | async-start | bytes 3145728 | tf_op jit(solution)/shard_map/psum | solution.py:197
Sparse Core Ops, SparseCore 0:
  218.8 93.6 all-reduce.1
where the time goes:
time: 323 us; the launch traced here: 322 us
  waiting for transfers between devices  194 us (60%)
  matrix products  43.6 us (13%)
  starting transfers between devices  22.6 us (7%)
  other arithmetic  21.4 us (7%)
  local copies, waits for them, and re-layouts  18.4 us (6%)
  between operations  14.4 us (4%)
  blocking collectives  7.93 us (2%)
    psum x1, waiting for transfers between devices, local(): lax.psum(feature_product(student_feats, top_part, rest_part), ('img', 'ca...  93.9 us
    all_to_all x1, waiting for transfers between devices, local(): lax.all_to_all(send_tokens.reshape(img_count, slot_count, length, itc_wid...  87.6 us
    dot_general x4, matrix products, pooled_scores(): jnp.einsum('rt,jt->rj', token_rows.reshape(-1, feature_width), query_rows...  39.4 us
    select_n x1, other arithmetic, local(): text_lens[source_caption][:, None]  9.95 us
    all_to_all x1, blocking collectives, local(): lax.all_to_all(send_grad.reshape(img_count, slot_count, BLOCK), 'img', sp...  7.93 us
  transfers between devices with their start and end apart: 6, of which 6 were waited for; matrix products, arithmetic and copies ran while one was open for 5% of the time, Pallas kernels for 0%

commit v1 on v0

v1 whole, which is shorter than its diff:
```python
import jax
import jax.numpy as jnp
from jax import lax
from jax.sharding import PartitionSpec as P

TEACHER_TEMP = 0.01
LOGIT_SCALE = 100.0
HIGHEST = lax.Precision.HIGHEST


def unit_rows(values):
    return values * lax.rsqrt(jnp.sum(values * values, axis=-1, keepdims=True) + 1e-06)


def local(
    text_states,
    text_lens,
    text_proj,
    query_states,
    vision_proj,
    student_text,
    student_feats,
    student_proj,
    candidates,
):
    cap_dev, length, txt_width = text_states.shape
    img_dev = query_states.shape[0]
    query_rows = unit_rows(
        jnp.dot(
            query_states.reshape(-1, txt_width), vision_proj, preferred_element_type=jnp.float32
        )
    ).astype(jnp.bfloat16)
    all_rows = lax.all_gather(query_rows, "img", axis=0, tiled=False)
    all_feats = lax.all_gather(student_feats, "img", axis=0, tiled=True)
    all_text = lax.all_gather(student_text, ("img", "cap"), axis=0, tiled=True)
    token_rows = unit_rows(
        jnp.dot(text_states.reshape(-1, txt_width), text_proj, preferred_element_type=jnp.float32)
    ).astype(jnp.bfloat16)
    img_count = lax.axis_size("img")
    images = img_count * img_dev

    valid_mask = jnp.arange(length)[None, :] < text_lens[:, None]
    pieces = []
    for owner in range(img_count):
        products = jnp.dot(
            token_rows, all_rows[owner].T, preferred_element_type=jnp.float32
        ).reshape(cap_dev, length, img_dev, -1)
        strongest = jnp.max(products, axis=-1)
        pieces.append(jnp.sum(jnp.where(valid_mask[:, :, None], strongest, 0.0), axis=1))
    summed = jnp.concatenate(pieces, axis=1)
    teacher = summed / text_lens[:, None].astype(jnp.float32) / TEACHER_TEMP

    image_embed = jnp.dot(all_feats, student_proj, preferred_element_type=jnp.float32)
    image_norm = jnp.sqrt(jnp.sum(image_embed * image_embed, axis=-1) + 1e-06)
    image_unit = image_embed / image_norm[:, None]
    text_unit = unit_rows(student_text.astype(jnp.float32))
    cosine = jnp.dot(text_unit, image_unit.T, precision=HIGHEST)
    student = LOGIT_SCALE * cosine

    counts = jnp.sum(
        (candidates[:, :, None] == jnp.arange(images)[None, None, :]).astype(jnp.float32), axis=1
    )
    present = counts > 0

    def log_softmax(scores):
        peak = jnp.max(jnp.where(present, scores, -jnp.inf), axis=1, keepdims=True)
        shifted = jnp.where(present, scores - peak, 0.0)
        total = jnp.sum(counts * jnp.exp(shifted), axis=1, keepdims=True)
        return shifted - jnp.log(total)

    teacher_log = log_softmax(teacher)
    student_log = log_softmax(student)
    teacher_prob = jnp.exp(teacher_log)
    losses = jnp.sum(counts * teacher_prob * (teacher_log - student_log), axis=1)
    spread = LOGIT_SCALE * counts * (jnp.exp(student_log) - teacher_prob)
    radial = jnp.sum(spread * cosine, axis=0, keepdims=True)
    all_spread = lax.all_gather(
        jnp.concatenate([spread, radial], axis=0), ("img", "cap"), axis=0, tiled=False
    )
    radial = jnp.sum(all_spread[:, cap_dev], axis=0)
    all_spread = all_spread[:, :cap_dev].reshape(-1, images)
    all_unit = unit_rows(all_text.astype(jnp.float32))
    embed_grad = (
        jnp.einsum("ci,cd->id", all_spread, all_unit, precision=HIGHEST)
        - radial[:, None] * image_unit
    ) / image_norm[:, None]
    top = lax.optimization_barrier(embed_grad.astype(jnp.bfloat16))
    rest = (embed_grad - top.astype(jnp.float32)).astype(jnp.bfloat16)
    proj_grad = jnp.einsum(
        "is,id->sd",
        jnp.concatenate([all_feats, all_feats], axis=0),
        jnp.concatenate([top, rest], axis=0),
        preferred_element_type=jnp.float32,
    )
    return (losses, proj_grad)


def solution(mesh):
    in_specs = (
        P(("groups", "img", "cap"), None, None),
        P(("groups", "img", "cap")),
        P(),
        P(("groups", "img"), None, None),
        P(),
        P(("groups", "img", "cap"), None),
        P(("groups", "img"), None),
        P(),
        P(("groups", "img", "cap"), None),
    )
    out_specs = (P(("groups", "img", "cap")), P("groups", None))
    return jax.shard_map(local, mesh=mesh, in_specs=in_specs, out_specs=out_specs, check_vma=False)
```

time: 323 us -> 95.7 us (0.30)
  waiting for transfers between devices: 194 us -> 0.02 us
  blocking collectives: 7.93 us -> 58 us
  matrix products: 43.6 us -> 12 us
  starting transfers between devices: 22.6 us -> 0.04 us
  local copies, waits for them, and re-layouts: 18.4 us -> 3.47 us
  other arithmetic: 21.4 us -> 7.62 us
    all_to_all x5 -> x0, waiting for transfers between devices: 100 us -> none  [the longest x1 87.6 us: local(): lax.all_to_all(send_tokens.reshape(img_count, slot_count, length, itc_wid...]
    psum x1 -> x0, waiting for transfers between devices: 93.9 us -> none  [local(): lax.psum(feature_product(student_feats, top_part, rest_part), ('img', 'ca...]
    all_gather x0 -> x3, blocking collectives: none -> 58 us  [the longest x1 24.6 us: local(): all_text = lax.all_gather(student_text, ('img', 'cap'), axis=0, tiled=True)]
    dot_general x9 -> x8, matrix products: 42.6 us -> 9.93 us  [the longest x4 6.35 us: local(): jnp.dot(token_rows, all_rows[owner].T, preferred_element_type=jnp.float32)]
    all_to_all x5 -> x0, starting transfers between devices: 22.5 us -> none  [the longest x1 6.32 us: local(): lax.all_to_all(send_meta.reshape(img_count, slot_count, BLOCK + 1), 'img'...]
    select_n x6 -> x0, other arithmetic: 14.8 us -> none  [the longest x1 9.95 us: local(): text_lens[source_caption][:, None]]
    gather x8 -> x0, local copies, waits for them, and re-layouts: 8.68 us -> none  [the longest x1 2.75 us: local(): token_rows[source_caption]]
    all_to_all x1 -> x0, blocking collectives: 7.93 us -> none  [local(): lax.all_to_all(send_grad.reshape(img_count, slot_count, BLOCK), 'img', sp...]
  transfers between devices with their start and end apart: 6 -> 1, of which waited for: 6 -> 0; matrix products, arithmetic and copies ran while one was open for 5% -> 7% of each run, Pallas kernels for 0% -> 0%
where the time goes in v1:
time: 95.7 us; the launch traced here: 95.5 us
  blocking collectives  58 us (61%)
  between operations  14.3 us (15%)
  matrix products  12 us (13%)
  other arithmetic  7.62 us (8%)
  local copies, waits for them, and re-layouts  3.47 us (4%)
    all_gather x1, blocking collectives, local(): all_text = lax.all_gather(student_text, ('img', 'cap'), axis=0, tiled=True)  24.6 us
    all_gather x1, blocking collectives, local(): lax.all_gather(jnp.concatenate([spread, radial], axis=0), ('img', 'cap'),...  18 us
    all_gather x1, blocking collectives, local(): all_feats = lax.all_gather(student_feats, 'img', axis=0, tiled=True)  15.4 us
    dot_general x4, matrix products, local(): jnp.dot(token_rows, all_rows[owner].T, preferred_element_type=jnp.float32)  6.35 us
    slice x5, local copies, waits for them, and re-layouts, local(): all_rows[owner]  2.14 us
  transfers between devices with their start and end apart: 1, of which 0 were waited for; matrix products, arithmetic and copies ran while one was open for 7% of the time, Pallas kernels for 0%

profile of v1, /device:TPU:0, one launch (start us, length us, event | category | flops | bytes accessed | tf_op | source)
XLA Modules:
  0.0 95.5 jit_solution(2823498708173622710)
XLA Ops:
  7.2 1.2 %copy-done = bf16[24,32,768]{2,1,0:T(8,128)(2,1)S(1)} copy-done((bf16[24,32,768]{2,1,0:T(8,128)(2,1)S(1)}, bf16[24,32,768]{2,1,0:T(8,128)(2,1)}, u32[]{:S(2)}) %copy-start) | copy-done | bytes 1179672
  8.5 1.6 %multiply_reduce_fusion = (f32[768]{0:T(1024)S(1)}, f32[768,256]{0,1:T(8,128)S(1)}) fusion(bf16[768,768]{1,0:T(8,128)(2,1)S(1)} %bitcast.38, bf16[768,256]{1,0:T(8,128)(2,1)} %param.13), kind=kOutput, calls=%fused_computation.7 | convolution fusion | flops 302382336 | bytes 2362368 | tf_op jit(solution)/shard_map/dot_general | solution.py:29
  10.1 0.8 multiply_convert_fusion
  10.9 0.5 convert_element_type.31
  11.4 15.4 %all_gather.20 = bf16[96,768]{1,0:T(8,128)(2,1)S(1)} all-gather(bf16[24,768]{1,0:T(8,128)(2,1)S(1)} %copy-done.11), channel_id=1, replica_groups=mesh['groups'=2,'img'=4,'cap'=4] {'img'}, dimensions={0}, use_global_device_ids=true | all-gather | bytes 184320 | tf_op jit(solution)/shard_map/all_gather | solution.py:34
  27.0 0.8 convert_reduce_fusion
  27.8 24.6 %all_gather.23 = bf16[256,512]{1,0:T(8,128)(2,1)S(1)} all-gather(bf16[16,512]{1,0:T(8,128)(2,1)} %param.14), channel_id=1, replica_groups=mesh['groups'=2,'img'=4,'cap'=4] {'img','cap'}, dimensions={0}, use_global_device_ids=true | all-gather | bytes 278528 | tf_op jit(solution)/shard_map/all_gather | solution.py:35
  52.5 0.1 fusion.1
  52.6 1.0 %multiply_reduce_fusion.2 = (f32[96]{0:T(128)S(1)}, f32[96,512]{1,0:T(8,128)}) fusion(bf16[96,768]{1,0:T(8,128)(2,1)S(1)} %all_gather.20, bf16[768,512]{1,0:T(8,128)(2,1)S(1)} %copy-done.1), kind=kOutput, calls=%fused_computation.24 | convolution fusion | flops 75595680 | bytes 1130880 | tf_op jit(solution)/shard_map/dot_general | solution.py:53
  53.6 0.5 add_sqrt_fusion
  54.2 0.5 add_rsqrt_fusion.3
  54.7 0.6 add_rsqrt_fusion.2
  55.3 1.3 %iota_compare_fusion.1 = pred[16,32]{1,0:T(8,128)(4,1)} fusion(s32[16]{0:T(128)} %param.10), kind=kLoop, calls=%fused_computation.48 | loop fusion | flops 512 | bytes 576 | tf_op jit(solution)/shard_map/lt | solution.py:42
  56.6 0.5 multiply_reduce_fusion.1
  57.1 0.9 multiply_convert_fusion.1
  57.9 1.5 %fusion.16 = (bf16[768,256]{0,1:T(8,128)(2,1)S(1)}, bf16[768,256]{0,1:T(8,128)(2,1)S(1)}, bf16[768,256]{0,1:T(8,128)(2,1)S(1)}, bf16[768,256]{0,1:T(8,128)(2,1)S(1)}) fusion(bf16[3072,256]{0,1:T(8,128)(2,1)} %all-gather.5.cloned.1.call-done), kind=kLoop, calls=%fused_computation.56 | loop fusion | bytes 3145728 | tf_op jit(solution)/shard_map/slice | solution.py:46
  59.4 0.2 copy.26
  59.6 0.2 copy.25
  59.7 2.7 %convolution_reduce_fusion = f32[16,32,24]{1,2,0:T(8,128)} fusion(bf16[16,32,256,1]{2,1,3,0:T(8,128)(2,1)} %bitcast.44, bf16[24,32,256,1]{2,1,0,3:T(8,128)(2,1)S(1)} %bitcast.40), kind=kOutput, calls=%fused_computation | convolution fusion | flops 201707520 | bytes 704512 | tf_op jit(solution)/shard_map/dot_general | solution.py:45
  62.4 1.7 %convolution_reduce_fusion.1 = f32[16,32,24]{1,2,0:T(8,128)} fusion(bf16[16,32,256,1]{2,1,3,0:T(8,128)(2,1)S(1)} %bitcast.45, bf16[24,32,256,1]{2,1,0,3:T(8,128)(2,1)S(1)} %bitcast.41), kind=kOutput, calls=%fused_computation.1 | convolution fusion | flops 201707520 | bytes 704512 | tf_op jit(solution)/shard_map/dot_general | solution.py:45
  64.1 0.2 copy.24
  64.3 1.0 %convolution_reduce_fusion.2 = f32[16,32,24]{1,2,0:T(8,128)S(1)} fusion(bf16[16,32,256,1]{2,1,3,0:T(8,128)(2,1)S(1)} %bitcast.46, bf16[24,32,256,1]{2,1,0,3:T(8,128)(2,1)S(1)} %bitcast.43), kind=kOutput, calls=%fused_computation.2 | convolution fusion | flops 201707520 | bytes 704512 | tf_op jit(solution)/shard_map/dot_general | solution.py:45
  65.3 0.2 copy.23
  65.5 1.0 %convolution_reduce_fusion.3 = f32[16,32,24]{1,2,0:T(8,128)S(1)} fusion(bf16[16,32,256,1]{2,1,3,0:T(8,128)(2,1)S(1)} %bitcast.47, bf16[24,32,256,1]{2,1,0,3:T(8,128)(2,1)S(1)} %bitcast.42), kind=kOutput, calls=%fused_computation.3 | convolution fusion | flops 201707520 | bytes 704512 | tf_op jit(solution)/shard_map/dot_general | solution.py:45
  66.6 0.3 select_reduce_fusion.3
  66.9 0.2 select_reduce_fusion.5
  67.1 0.5 multiply_reduce_fusion.6
  67.6 0.2 multiply_reduce_fusion.5
  67.8 0.7 multiply_reduce_fusion.3
  68.5 18.0 %all-gather.2 = f32[16,17,96]{2,1,0:T(8,128)S(1)} all-gather(f32[1,17,96]{2,1,0:T(8,128)S(1)} %maximum_bitcast_fusion), channel_id=3, replica_groups=mesh['groups'=2,'img'=4,'cap'=4] {'img','cap'}, dimensions={0}, use_global_device_ids=true | all-gather | bytes 110976 | tf_op jit(solution)/shard_map/all_gather | solution.py:77
  86.5 0.5 fusion.17
  87.1 1.6 %fusion.2 = f32[768,512]{1,0:T(8,128)} fusion(bf16[96,768]{1,0:T(8,128)(2,1)S(1)} %all_gather.20, bf16[96,512]{1,0:T(8,128)(2,1)S(1)} %subtract_convert_fusion, bf16[96,512]{1,0:T(8,128)(2,1)S(1)} %get-tuple-element.24), kind=kOutput, calls=%fused_computation.15 | convolution fusion | flops 151977984 | bytes 1916928 | tf_op jit(solution)/shard_map/is,id->sd/dot_general | solution.py:89
  (49 shorter events, 0.4 us)
Async XLA Ops:
  7.2 1.3 %copy-start = (bf16[24,32,768]{2,1,0:T(8,128)(2,1)S(1)}, bf16[24,32,768]{2,1,0:T(8,128)(2,1)}, u32[]{:S(2)}) copy-start(bf16[24,32,768]{2,1,0:T(8,128)(2,1)} %param.12) | copy-start | bytes 3538948
  7.2 50.7 %all-gather.5.cloned.1.call-start = ((), (), s32[]{:S(2)}) async-start(), calls=%async_computation | async-start | bytes 1966080 | tf_op jit(solution)/shard_map/all_gather | solution.py:33
  8.4 2.5 %copy-start.16 = (s32[16]{0:T(128)S(1)}, s32[16]{0:T(128)}, u32[]{:S(2)}) copy-start(s32[16]{0:T(128)} %param.10) | copy-start | bytes 196
  8.4 3.0 %copy-start.11 = (bf16[24,768]{1,0:T(8,128)(2,1)S(1)}, bf16[24,768]{1,0:T(8,128)(2,1)}, u32[]{:S(2)}) copy-start(bf16[24,768]{1,0:T(8,128)(2,1)} %param.15) | copy-start | bytes 110596
  8.4 18.4 %copy-start.9 = (bf16[16,512]{1,0:T(8,128)(2,1)S(1)}, bf16[16,512]{1,0:T(8,128)(2,1)}, u32[]{:S(2)}) copy-start(bf16[16,512]{1,0:T(8,128)(2,1)} %param.14) | copy-start | bytes 49156
  8.4 18.6 %copy-start.13 = (s32[16,64]{1,0:T(8,128)S(1)}, s32[16,64]{1,0:T(8,128)}, u32[]{:S(2)}) copy-start(s32[16,64]{1,0:T(8,128)} %param.17) | copy-start | bytes 12292
  10.0 42.5 %copy-start.1 = (bf16[768,512]{1,0:T(8,128)(2,1)S(1)}, bf16[768,512]{1,0:T(8,128)(2,1)}, u32[]{:S(2)}) copy-start(bf16[768,512]{1,0:T(8,128)(2,1)} %param.16) | copy-start | bytes 2359300
  10.1 46.5 %copy-start.2 = (bf16[16,32,768]{2,1,0:T(8,128)(2,1)S(1)}, bf16[16,32,768]{2,1,0:T(8,128)(2,1)}, u32[]{:S(2)}) copy-start(bf16[16,32,768]{2,1,0:T(8,128)(2,1)} %param.9) | copy-start | bytes 2359300
  10.1 46.5 %copy-start.3 = (bf16[768,256]{1,0:T(8,128)(2,1)S(1)}, bf16[768,256]{1,0:T(8,128)(2,1)}, u32[]{:S(2)}) copy-start(bf16[768,256]{1,0:T(8,128)(2,1)} %param.11) | copy-start | bytes 1179652
  59.7 2.7 %copy-start.4 = (bf16[512,256]{1,0:T(8,128)(2,1)S(1)}, bf16[512,256]{1,0:T(8,128)(2,1)}, u32[]{:S(2)}) copy-start(bf16[512,256]{1,0:T(8,128)(2,1)} %multiply_convert_fusion.1) | copy-start | bytes 786436
  65.4 1.1 %copy-start.5 = (f32[16,32,24]{1,2,0:T(8,128)S(1)}, f32[16,32,24]{1,2,0:T(8,128)}, u32[]{:S(2)}) copy-start(f32[16,32,24]{1,2,0:T(8,128)} %convolution_reduce_fusion) | copy-start | bytes 147460
  65.5 1.1 %copy-start.6 = (f32[16,32,24]{1,2,0:T(8,128)S(1)}, f32[16,32,24]{1,2,0:T(8,128)}, u32[]{:S(2)}) copy-start(f32[16,32,24]{1,2,0:T(8,128)} %convolution_reduce_fusion.1) | copy-start | bytes 147460
  65.5 1.1 %copy-start.12 = (pred[16,32]{1,0:T(8,128)(4,1)S(1)}, pred[16,32]{1,0:T(8,128)(4,1)}, u32[]{:S(2)}) copy-start(pred[16,32]{1,0:T(8,128)(4,1)} %iota_compare_fusion.1) | copy-start | bytes 1540
  65.5 1.4 %copy-start.8 = (f32[16,96]{1,0:T(8,128)S(1)}, f32[16,96]{1,0:T(8,128)}, u32[]{:S(2)}) copy-start(f32[16,96]{1,0:T(8,128)} %convert_reduce_fusion) | copy-start | bytes 18436
  65.5 1.4 %copy-start.15 = (f32[16]{0:T(128)S(1)}, f32[16]{0:T(128)}, u32[]{:S(2)}) copy-start(f32[16]{0:T(128)} %convert_element_type.31) | copy-start | bytes 196
  65.5 1.6 %copy-start.7 = (f32[96,512]{1,0:T(8,128)S(1)}, f32[96,512]{1,0:T(8,128)}, u32[]{:S(2)}) copy-start(f32[96,512]{1,0:T(8,128)} %get-tuple-element.18) | copy-start | bytes 589828
  65.5 1.6 %copy-start.10 = (bf16[16,512]{1,0:T(8,128)(2,1)S(1)}, bf16[16,512]{1,0:T(8,128)(2,1)}, u32[]{:S(2)}) copy-start(bf16[16,512]{1,0:T(8,128)(2,1)} %param.14) | copy-start | bytes 49156
  65.5 1.6 %copy-start.17 = (f32[96]{0:T(128)S(1)}, f32[96]{0:T(128)}, u32[]{:S(2)}) copy-start(f32[96]{0:T(128)} %add_sqrt_fusion) | copy-start | bytes 1156
  65.5 1.6 %copy-start.18 = (f32[16]{0:T(128)S(1)}, f32[16]{0:T(128)}, u32[]{:S(2)}) copy-start(f32[16]{0:T(128)} %add_rsqrt_fusion.3) | copy-start | bytes 196
  66.6 20.0 %copy-start.14 = (f32[256]{0:T(256)S(1)}, f32[256]{0:T(256)}, u32[]{:S(2)}) copy-start(f32[256]{0:T(256)} %add_rsqrt_fusion.2) | copy-start | bytes 3076
Sparse Core Ops, SparseCore 0:
  11.0 41.2 all-gather.4

commit v2 on v1

--- a/solution.py
+++ b/solution.py
@@ -1,6 +1,8 @@
 import jax
 import jax.numpy as jnp
 from jax import lax
+from jax.experimental import pallas as pl
+from jax.experimental.pallas import tpu as pltpu
 from jax.sharding import PartitionSpec as P
 
 TEACHER_TEMP = 0.01
@@ -12,7 +14,7 @@
     return values * lax.rsqrt(jnp.sum(values * values, axis=-1, keepdims=True) + 1e-06)
 
 
-def local(
+def gathered(
     text_states,
     text_lens,
     text_proj,
@@ -95,7 +97,345 @@
     return (losses, proj_grad)
 
 
+MESH = pl.DeviceIdType.MESH
+LAST = (((1,), (1,)), ((), ()))
+NEAR_FIRST = (1, 3, 2)
+
+
+def split_three(values):
+    top = values.astype(jnp.bfloat16)
+    rest = values - top.astype(jnp.float32)
+    middle = rest.astype(jnp.bfloat16)
+    low = (rest - middle.astype(jnp.float32)).astype(jnp.bfloat16)
+    return (top, middle, low)
+
+
+def product_three(exact, values):
+    rows = values.shape[0]
+    stacked = jnp.concatenate(split_three(values), axis=0)
+    found = lax.dot_general(exact, stacked, LAST, preferred_element_type=jnp.float32)
+    return found[:, :rows] + found[:, rows : 2 * rows] + found[:, 2 * rows :]
+
+
+def fused_kernel(
+    lens_ref,
+    cand_ref,
+    text_ref,
+    feats_ref,
+    states_hbm,
+    tproj_hbm,
+    query_hbm,
+    vproj_hbm,
+    sproj_hbm,
+    losses_ref,
+    grad_ref,
+    feats_out_ref,
+    states,
+    tproj,
+    query,
+    vproj,
+    sproj,
+    packs,
+    own_rows,
+    tokens,
+    strong,
+    spreads,
+    feats_all,
+    text_all,
+    load_sem,
+    send_sem,
+    recv_sem,
+    spread_send,
+    spread_recv,
+):
+    n_img, n_cap = packs.shape[:2]
+    cap_dev, length, width = states.shape
+    img_dev, queries = query.shape[:2]
+    part_img = img_dev // n_cap
+    part_rows = part_img * queries
+    itc = tokens.shape[1]
+    slots = n_img * n_cap * 8
+    text_at, feat_at = (part_rows, part_rows + 32)
+    i, j = (lax.axis_index("img"), lax.axis_index("cap"))
+    chip, core = (j // 2, j % 2)
+    sibling = 2 * chip + (1 - core)
+    across = 2 * (1 - chip) + core
+    corner = 2 * (1 - chip) + (1 - core)
+
+    loads = []
+    for index, (hbm, vmem) in enumerate(
+        (
+            (query_hbm, query),
+            (vproj_hbm, vproj),
+            (states_hbm, states),
+            (tproj_hbm, tproj),
+            (sproj_hbm, sproj),
+        )
+    ):
+        loads.append(pltpu.make_async_copy(hbm, vmem, load_sem.at[index]))
+        loads[-1].start()
+
+    barrier = pltpu.get_barrier_semaphore()
+    for step in range(1, n_img * n_cap):
+        peer = {"img": (i + step // n_cap) % n_img, "cap": (j + step % n_cap) % n_cap}
+        pl.semaphore_signal(barrier, inc=1, device_id=peer, device_id_type=MESH)
+
+    def remote(source, target, kind, step, to_img, to_cap):
+        return pltpu.make_async_remote_copy(
+            src_ref=source,
+            dst_ref=target,
+            send_sem=send_sem.at[kind, step],
+            recv_sem=recv_sem.at[kind, step],
+            device_id={"img": to_img, "cap": to_cap},
+            device_id_type=MESH,
+        )
+
+    mine = packs.at[i, j]
+    text = text_ref[...]
+    mine[pl.ds(text_at, 16), :] = text[:, :itc]
+    mine[pl.ds(text_at + 16, 16), :] = text[:, itc:]
+    row = lax.broadcasted_iota(jnp.int32, (n_cap * 8, img_dev), 0)
+    column = lax.broadcasted_iota(jnp.int32, (n_cap * 8, img_dev), 1)
+    wanted = jnp.where(row % 8 < part_img, (row // 8) * part_img + row % 8, -1)
+    chooser = (column == wanted).astype(jnp.bfloat16)
+    placed = jnp.dot(chooser, feats_ref[...], preferred_element_type=jnp.float32).astype(
+        jnp.bfloat16
+    )
+    feats_all[pl.ds(pl.multiple_of(i * n_cap * 8, n_cap * 8), n_cap * 8), :] = placed
+    for part in range(n_cap):
+        begin = itc * min(part, width // itc - 1)
+
+        @pl.when(j == part)
+        def _():
+            mine[pl.ds(feat_at, 32), :] = placed[:, begin : begin + itc]
+
+    loads[0].wait()
+    loads[1].wait()
+    own_rows[...] = unit_rows(
+        jnp.dot(
+            query[...].reshape(img_dev * queries, width),
+            vproj[...],
+            preferred_element_type=jnp.float32,
+        )
+    ).astype(jnp.bfloat16)
+    mine[pl.ds(0, part_rows), :] = own_rows[
+        pl.ds(pl.multiple_of(j * part_rows, part_rows), part_rows), :
+    ]
+    pl.semaphore_wait(barrier, n_img * n_cap - 1)
+
+    along = {}
+    for step in NEAR_FIRST:
+        along[step] = remote(mine, mine, 0, step, (i + step) % n_img, j)
+        along[step].start()
+    texts = {}
+    for step, peer in ((1, sibling), (2, across), (3, corner)):
+        piece = mine.at[pl.ds(text_at, 32), :]
+        texts[step] = remote(piece, piece, 4, step, i, peer)
+        texts[step].start()
+
+    loads[2].wait()
+    loads[3].wait()
+    tokens[...] = unit_rows(
+        jnp.dot(
+            states[...].reshape(cap_dev * length, width),
+            tproj[...],
+            preferred_element_type=jnp.float32,
+        )
+    ).astype(jnp.bfloat16)
+    strong[...] = jnp.zeros_like(strong)
+
+    def score(rows, owner, part):
+        products = lax.dot_general(rows, tokens[...], LAST, preferred_element_type=jnp.float32)
+        strong[owner * n_cap + part, :part_img, :] = jnp.max(
+            products.reshape(part_img, queries, cap_dev * length), axis=1
+        )
+
+    for part in range(n_cap):
+        score(own_rows[pl.ds(part * part_rows, part_rows), :], i, part)
+
+    slot = lax.broadcasted_iota(jnp.int32, (cap_dev, slots), 1)
+    image = jnp.where(slot % 8 < part_img, (slot // 8) * part_img + slot % 8, -1)
+    counts = jnp.zeros((cap_dev, slots), jnp.float32)
+    cand = cand_ref[...]
+    for k in range(cand.shape[1]):
+        counts += (cand[:, k : k + 1] == image).astype(jnp.float32)
+    caption = lax.broadcasted_iota(jnp.int32, (cap_dev, 1), 0)
+    lens = jnp.zeros((cap_dev, 1), jnp.int32)
+    for c in range(cap_dev):
+        lens = jnp.where(caption == c, lens_ref[c], lens)
+    place = lax.broadcasted_iota(jnp.int32, (cap_dev, cap_dev * length), 1)
+    at = place - caption * length
+    mask = ((at >= 0) & (at < lens)).astype(jnp.bfloat16)
+
+    def use_text(owner, part):
+        begin = pl.multiple_of((owner * n_cap + part) * 16, 16)
+        text_all[pl.ds(begin, 16), :itc] = packs[owner, part, pl.ds(text_at, 16), :]
+        text_all[pl.ds(begin, 16), itc:] = packs[owner, part, pl.ds(text_at + 16, 16), :]
+
+    def use(owner, part):
+        score(packs[owner, part, pl.ds(0, part_rows), :], owner, part)
+        use_text(owner, part)
+        rows = pl.ds(pl.multiple_of(owner * n_cap * 8, n_cap * 8), n_cap * 8)
+        begin = pl.multiple_of(jnp.minimum(part, width // itc - 1) * itc, itc)
+        feats_all[rows, pl.ds(begin, itc)] = packs[owner, part, pl.ds(feat_at, 32), :]
+
+    over, beside, onward = ({}, {}, {})
+    for step in NEAR_FIRST:
+        owner = (i - step + n_img) % n_img
+        along[step].wait_recv()
+        block = packs.at[owner, j]
+        over[step] = remote(block, block, 1, step, i, across)
+        over[step].start()
+        beside[step] = remote(block, block, 2, step, i, sibling)
+        beside[step].start()
+        use(owner, j)
+    use_text(i, j)
+    for step, peer in ((1, sibling), (2, across), (3, corner)):
+        texts[step].wait_recv()
+        use_text(i, peer)
+    for step in NEAR_FIRST:
+        owner = (i - step + n_img) % n_img
+        over[step].wait_recv()
+        block = packs.at[owner, across]
+        onward[step] = remote(block, block, 3, step, i, sibling)
+        onward[step].start()
+        use(owner, across)
+        beside[step].wait_recv()
+        use(owner, sibling)
+    for step in NEAR_FIRST:
+        onward[step].wait_recv()
+        use((i - step + n_img) % n_img, corner)
+
+    loads[4].wait()
+    embed = jnp.dot(feats_all[...], sproj[...], preferred_element_type=jnp.float32)
+    norm = jnp.sqrt(jnp.sum(embed * embed, axis=-1, keepdims=True) + 1e-06)
+    unit = embed / norm
+    wide = text.astype(jnp.float32)
+    text_scale = lax.rsqrt(jnp.sum(wide * wide, axis=-1, keepdims=True) + 1e-06)
+    student = LOGIT_SCALE * (product_three(text, unit) * text_scale)
+    summed = product_three(mask, strong[...].reshape(slots, cap_dev * length))
+    teacher = summed / lens.astype(jnp.float32) / TEACHER_TEMP
+    present = counts > 0
+
+    def log_softmax(scores):
+        peak = jnp.max(jnp.where(present, scores, -jnp.inf), axis=1, keepdims=True)
+        shifted = jnp.where(present, scores - peak, 0.0)
+        total = jnp.sum(counts * jnp.exp(shifted), axis=1, keepdims=True)
+        return shifted - jnp.log(total)
+
+    teacher_log = log_softmax(teacher)
+    student_log = log_softmax(student)
+    teacher_prob = jnp.exp(teacher_log)
+    spreads[i, j] = (LOGIT_SCALE * text_scale) * (counts * (jnp.exp(student_log) - teacher_prob))
+    sent = []
+    for step in range(1, n_img * n_cap):
+        sent.append(
+            pltpu.make_async_remote_copy(
+                src_ref=spreads.at[i, j],
+                dst_ref=spreads.at[i, j],
+                send_sem=spread_send.at[step],
+                recv_sem=spread_recv.at[step],
+                device_id={
+                    "img": (i + step // n_cap) % n_img,
+                    "cap": (j + step % n_cap) % n_cap,
+                },
+                device_id_type=MESH,
+            )
+        )
+        sent[-1].start()
+    losses_ref[...] = jnp.sum(
+        counts * teacher_prob * (teacher_log - student_log), axis=1, keepdims=True
+    )
+    turned = feats_all[...].astype(jnp.float32).T.astype(jnp.bfloat16)
+    feats_out_ref[:, :slots] = turned
+    feats_out_ref[:, slots:] = turned
+    for copies in (along, over, beside, onward, texts):
+        for step in NEAR_FIRST:
+            copies[step].wait_send()
+    for copy in sent:
+        copy.wait_recv()
+    across_captions = spreads[...].reshape(n_img * n_cap * cap_dev, slots).T
+    total = jnp.zeros(embed.shape, jnp.float32)
+    for piece in split_three(across_captions):
+        total += jnp.dot(piece, text_all[...], preferred_element_type=jnp.float32)
+    radial = jnp.sum(total * unit, axis=-1, keepdims=True)
+    embed_grad = (total - radial * unit) / norm
+    top = embed_grad.astype(jnp.bfloat16)
+    grad_ref[:slots, :] = top
+    grad_ref[slots:, :] = (embed_grad - top.astype(jnp.float32)).astype(jnp.bfloat16)
+    for copy in sent:
+        copy.wait_send()
+
+
+def fused(
+    text_states,
+    text_lens,
+    text_proj,
+    query_states,
+    vision_proj,
+    student_text,
+    student_feats,
+    student_proj,
+    candidates,
+):
+    n_img, n_cap = (lax.axis_size("img"), lax.axis_size("cap"))
+    cap_dev, length, width = text_states.shape
+    img_dev, queries = query_states.shape[:2]
+    itc = text_proj.shape[1]
+    embed_width = student_proj.shape[1]
+    slots = n_img * n_cap * 8
+    part_rows = img_dev * queries // n_cap
+    vmem = pl.BlockSpec(memory_space=pltpu.VMEM)
+    anywhere = pl.BlockSpec(memory_space=pl.ANY)
+    losses, grads, feats = pl.pallas_call(
+        fused_kernel,
+        out_shape=(
+            jax.ShapeDtypeStruct((cap_dev, 1), jnp.float32),
+            jax.ShapeDtypeStruct((2 * slots, embed_width), jnp.bfloat16),
+            jax.ShapeDtypeStruct((width, 2 * slots), jnp.bfloat16),
+        ),
+        in_specs=[pl.BlockSpec(memory_space=pltpu.SMEM)] + [vmem] * 3 + [anywhere] * 5,
+        out_specs=(vmem, vmem, vmem),
+        scratch_shapes=[
+            pltpu.VMEM(text_states.shape, jnp.bfloat16),
+            pltpu.VMEM(text_proj.shape, jnp.bfloat16),
+            pltpu.VMEM(query_states.shape, jnp.bfloat16),
+            pltpu.VMEM(vision_proj.shape, jnp.bfloat16),
+            pltpu.VMEM(student_proj.shape, jnp.bfloat16),
+            pltpu.VMEM((n_img, n_cap, part_rows + 64, itc), jnp.bfloat16),
+            pltpu.VMEM((img_dev * queries, itc), jnp.bfloat16),
+            pltpu.VMEM((cap_dev * length, itc), jnp.bfloat16),
+            pltpu.VMEM((n_img * n_cap, 8, cap_dev * length), jnp.float32),
+            pltpu.VMEM((n_img, n_cap, cap_dev, slots), jnp.float32),
+            pltpu.VMEM((slots, width), jnp.bfloat16),
+            pltpu.VMEM((n_img * n_cap * cap_dev, embed_width), jnp.bfloat16),
+            pltpu.SemaphoreType.DMA((5,)),
+            pltpu.SemaphoreType.DMA((5, 4)),
+            pltpu.SemaphoreType.DMA((5, 4)),
+            pltpu.SemaphoreType.DMA((n_img * n_cap,)),
+            pltpu.SemaphoreType.DMA((n_img * n_cap,)),
+        ],
+        compiler_params=pltpu.CompilerParams(
+            collective_id=0, has_side_effects=True, vmem_limit_bytes=48 * 1024 * 1024
+        ),
+    )(
+        text_lens,
+        candidates,
+        student_text,
+        student_feats,
+        text_states,
+        text_proj,
+        query_states,
+        vision_proj,
+        student_proj,
+    )
+    proj_grad = jnp.dot(feats, grads, preferred_element_type=jnp.float32)
+    return (losses.reshape(cap_dev), proj_grad)
+
+
 def solution(mesh):
+    small = mesh.shape["img"] == 4 and mesh.shape["cap"] == 4
+    local = fused if small else gathered
     in_specs = (
         P(("groups", "img", "cap"), None, None),
         P(("groups", "img", "cap")),

time: 95.7 us -> 44.2 us (0.46)
  blocking collectives: 58 us -> 0 us
  Pallas kernels: 0 us -> 32.6 us
  between operations: 14.3 us -> 0.66 us
  matrix products: 12 us -> 1.5 us
  other arithmetic: 7.62 us -> 0.63 us
  local copies, waits for them, and re-layouts: 3.47 us -> 8.35 us
    all_gather x3 -> x0, blocking collectives: 58 us -> none  [the longest x1 24.6 us: local(): all_text = lax.all_gather(student_text, ('img', 'cap'), axis=0, tiled=True)]
    pallas_call x0 -> x1, Pallas kernels: none -> 32.6 us  [fused(): pl.pallas_call(fused_kernel, out_shape=(jax.ShapeDtypeStruct((cap_dev, 1)...]
    dot_general x10 -> x1, matrix products: 12 us -> 1.5 us  [fused(): proj_grad = jnp.dot(feats, grads, preferred_element_type=jnp.float32)]
    unnamed x38 -> x18, local copies, waits for them, and re-layouts: 1.31 us -> 8.35 us
    reduce_sum x7 -> x0, other arithmetic: 2.27 us -> none  [the longest x1 0.81 us: local(): jnp.sum((candidates[:, :, None] == jnp.arange(images)[None, None, :]).ast...]
    convert_element_type x4 -> x0, other arithmetic: 2.18 us -> none  [the longest x1 0.85 us: local(): token_rows = unit_rows(jnp.dot(text_states.reshape(-1, txt_width), text_p...]
    slice x6 -> x0, local copies, waits for them, and re-layouts: 2.15 us -> none  [the longest x5 2.14 us: local(): all_rows[owner]]
    lt x1 -> x0, other arithmetic: 1.31 us -> none  [local(): valid_mask = jnp.arange(length)[None, :] < text_lens[:, None]]
  transfers between devices with their start and end apart: 1 -> 0, of which waited for: 0 -> 0; matrix products, arithmetic and copies ran while one was open for 7% -> 0% of each run, Pallas kernels for 0% -> 0%
where the time goes in v2:
time: 44.2 us; the launch traced here: 43.7 us
  Pallas kernels  32.6 us (74%)
  local copies, waits for them, and re-layouts  8.35 us (19%)
  matrix products  1.5 us (3%)
  between operations  0.66 us (1%)
  other arithmetic  0.63 us (1%)
    pallas_call x1, Pallas kernels, fused(): pl.pallas_call(fused_kernel, out_shape=(jax.ShapeDtypeStruct((cap_dev, 1)...  32.6 us
    unnamed x18, local copies, waits for them, and re-layouts  8.35 us
    dot_general x1, matrix products, fused(): proj_grad = jnp.dot(feats, grads, preferred_element_type=jnp.float32)  1.5 us

profile of v2, /device:TPU:0, one launch (start us, length us, event | category | flops | bytes accessed | tf_op | source)
XLA Modules:
  0.0 43.7 jit_solution(443803033713721716)
XLA Ops:
  0.6 0.0 copy-start
  0.6 1.3 %copy-done = bf16[24,32,768]{2,1,0:T(8,128)(2,1)S(1)} copy-done((bf16[24,32,768]{2,1,0:T(8,128)(2,1)S(1)}, bf16[24,32,768]{2,1,0:T(8,128)(2,1)}, u32[]{:S(2)}) %copy-start) | copy-done | bytes 1179672
  1.9 0.0 copy-start.1
  1.9 1.1 %copy-done.1 = bf16[16,32,768]{2,1,0:T(8,128)(2,1)S(1)} copy-done((bf16[16,32,768]{2,1,0:T(8,128)(2,1)S(1)}, bf16[16,32,768]{2,1,0:T(8,128)(2,1)}, u32[]{:S(2)}) %copy-start.1) | copy-done | bytes 786456
  3.0 0.0 copy-start.2
  3.0 1.1 %copy-done.2 = bf16[768,512]{1,0:T(8,128)(2,1)S(1)} copy-done((bf16[768,512]{1,0:T(8,128)(2,1)S(1)}, bf16[768,512]{1,0:T(8,128)(2,1)}, u32[]{:S(2)}) %copy-start.2) | copy-done | bytes 786456
  4.2 0.0 copy-start.3
  4.2 1.0 %copy-done.3 = bf16[768,256]{1,0:T(8,128)(2,1)S(1)} copy-done((bf16[768,256]{1,0:T(8,128)(2,1)S(1)}, bf16[768,256]{1,0:T(8,128)(2,1)}, u32[]{:S(2)}) %copy-start.3) | copy-done | bytes 393240
  5.2 0.0 copy-start.4
  5.2 1.0 %copy-done.4 = bf16[768,256]{1,0:T(8,128)(2,1)S(1)} copy-done((bf16[768,256]{1,0:T(8,128)(2,1)S(1)}, bf16[768,256]{1,0:T(8,128)(2,1)}, u32[]{:S(2)}) %copy-start.4) | copy-done | bytes 393240
  6.2 0.0 copy-start.5
  6.2 0.8 %copy-done.5 = bf16[24,768]{1,0:T(8,128)(2,1)S(1)} copy-done((bf16[24,768]{1,0:T(8,128)(2,1)S(1)}, bf16[24,768]{1,0:T(8,128)(2,1)}, u32[]{:S(2)}) %copy-start.5) | copy-done | bytes 36888
  6.9 0.0 copy-start.6
  6.9 0.7 %copy-done.6 = bf16[16,512]{1,0:T(8,128)(2,1)S(1)} copy-done((bf16[16,512]{1,0:T(8,128)(2,1)S(1)}, bf16[16,512]{1,0:T(8,128)(2,1)}, u32[]{:S(2)}) %copy-start.6) | copy-done | bytes 16408
  7.7 0.0 copy-start.7
  7.7 0.7 %copy-done.7 = s32[16,64]{1,0:T(8,128)S(1)} copy-done((s32[16,64]{1,0:T(8,128)S(1)}, s32[16,64]{1,0:T(8,128)}, u32[]{:S(2)}) %copy-start.7) | copy-done | bytes 4120
  8.3 0.0 copy-start.8
  8.4 0.7 %copy-done.8 = s32[16]{0:T(128)S(1)} copy-done((s32[16]{0:T(128)S(1)}, s32[16]{0:T(128)}, u32[]{:S(2)}) %copy-start.8) | copy-done | bytes 88
  9.0 32.6 %shard_map.104 = (f32[16,1]{1,0:T(8,128)S(1)}, bf16[256,512]{1,0:T(8,128)(2,1)S(1)}, bf16[768,256]{1,0:T(8,128)(2,1)S(1)}) custom-call(s32[16]{0:T(128)S(1)} %copy-done.8, s32[16,64]{1,0:T(8,128)S(1)} %copy-done.7, bf16[16,512]{1,0:T(8,128)(2,1)S(1)} %copy-done.6, bf16[24,768]{1,0:T(8,128)(2,1)S(1)} %copy-done.5, bf16[16,32,768]{2,1,0:T(8,128)(2,1)S(1)} %copy-done.1, ...), custom_call_target="tpu_custom_call" | custom-call | tf_op jit(solution)/shard_map/pallas_call | solution.py:390
  41.6 0.6 %reduce = f32[16]{0:T(128)} reduce(f32[16,1]{1,0:T(8,128)S(1)} %get-tuple-element.5, f32[]{:T(128)} %constant.4), dimensions={1}, to_apply=%get-tuple-element.5.reduce_sub_computation | reduce | bytes 132 | tf_op jit(solution)/shard_map/pallas_call | solution.py:390
  42.2 1.5 %fusion = f32[768,512]{1,0:T(8,128)} fusion(bf16[768,256]{1,0:T(8,128)(2,1)S(1)} %get-tuple-element.6, bf16[256,512]{1,0:T(8,128)(2,1)S(1)} %get-tuple-element.7), kind=kOutput, calls=%fused_computation | convolution fusion | flops 201326592 | bytes 2228224 | tf_op jit(solution)/shard_map/dot_general | solution.py:432
Async XLA Ops:
  0.6 1.3 %copy-start = (bf16[24,32,768]{2,1,0:T(8,128)(2,1)S(1)}, bf16[24,32,768]{2,1,0:T(8,128)(2,1)}, u32[]{:S(2)}) copy-start(bf16[24,32,768]{2,1,0:T(8,128)(2,1)} %query_hbm.1) | copy-start | bytes 3538948
  1.9 1.1 %copy-start.1 = (bf16[16,32,768]{2,1,0:T(8,128)(2,1)S(1)}, bf16[16,32,768]{2,1,0:T(8,128)(2,1)}, u32[]{:S(2)}) copy-start(bf16[16,32,768]{2,1,0:T(8,128)(2,1)} %states_hbm.1) | copy-start | bytes 2359300
  3.0 1.1 %copy-start.2 = (bf16[768,512]{1,0:T(8,128)(2,1)S(1)}, bf16[768,512]{1,0:T(8,128)(2,1)}, u32[]{:S(2)}) copy-start(bf16[768,512]{1,0:T(8,128)(2,1)} %sproj_hbm.1) | copy-start | bytes 2359300
  4.2 1.0 %copy-start.3 = (bf16[768,256]{1,0:T(8,128)(2,1)S(1)}, bf16[768,256]{1,0:T(8,128)(2,1)}, u32[]{:S(2)}) copy-start(bf16[768,256]{1,0:T(8,128)(2,1)} %tproj_hbm.1) | copy-start | bytes 1179652
  5.2 1.0 %copy-start.4 = (bf16[768,256]{1,0:T(8,128)(2,1)S(1)}, bf16[768,256]{1,0:T(8,128)(2,1)}, u32[]{:S(2)}) copy-start(bf16[768,256]{1,0:T(8,128)(2,1)} %vproj_hbm.1) | copy-start | bytes 1179652
  6.2 0.8 %copy-start.5 = (bf16[24,768]{1,0:T(8,128)(2,1)S(1)}, bf16[24,768]{1,0:T(8,128)(2,1)}, u32[]{:S(2)}) copy-start(bf16[24,768]{1,0:T(8,128)(2,1)} %feats_ref.1) | copy-start | bytes 110596
  6.9 0.7 %copy-start.6 = (bf16[16,512]{1,0:T(8,128)(2,1)S(1)}, bf16[16,512]{1,0:T(8,128)(2,1)}, u32[]{:S(2)}) copy-start(bf16[16,512]{1,0:T(8,128)(2,1)} %text_ref.1) | copy-start | bytes 49156
  7.7 0.7 %copy-start.7 = (s32[16,64]{1,0:T(8,128)S(1)}, s32[16,64]{1,0:T(8,128)}, u32[]{:S(2)}) copy-start(s32[16,64]{1,0:T(8,128)} %cand_ref.1) | copy-start | bytes 12292
  8.3 0.7 %copy-start.8 = (s32[16]{0:T(128)S(1)}, s32[16]{0:T(128)}, u32[]{:S(2)}) copy-start(s32[16]{0:T(128)} %lens_ref.1) | copy-start | bytes 196

commit v3 on v2

--- a/solution.py
+++ b/solution.py
@@ -99,7 +99,7 @@
 
 MESH = pl.DeviceIdType.MESH
 LAST = (((1,), (1,)), ((), ()))
-NEAR_FIRST = (1, 3, 2)
+STEPS = (1, 2, 3)
 
 
 def split_three(values):
@@ -118,24 +118,30 @@
 
 
 def fused_kernel(
-    lens_ref,
-    cand_ref,
-    text_ref,
-    feats_ref,
     states_hbm,
+    lens_hbm,
     tproj_hbm,
     query_hbm,
     vproj_hbm,
+    text_hbm,
+    feats_hbm,
     sproj_hbm,
+    cand_hbm,
     losses_ref,
     grad_ref,
     feats_out_ref,
     states,
+    lens_ref,
     tproj,
     query,
     vproj,
+    text_ref,
+    feats_ref,
     sproj,
+    cand_ref,
+    quarter,
     packs,
+    sides,
     own_rows,
     tokens,
     strong,
@@ -155,45 +161,55 @@
     part_rows = part_img * queries
     itc = tokens.shape[1]
     slots = n_img * n_cap * 8
-    text_at, feat_at = (part_rows, part_rows + 32)
     i, j = (lax.axis_index("img"), lax.axis_index("cap"))
     chip, core = (j // 2, j % 2)
     sibling = 2 * chip + (1 - core)
     across = 2 * (1 - chip) + core
     corner = 2 * (1 - chip) + (1 - core)
-
-    loads = []
-    for index, (hbm, vmem) in enumerate(
-        (
-            (query_hbm, query),
-            (vproj_hbm, vproj),
-            (states_hbm, states),
-            (tproj_hbm, tproj),
-            (sproj_hbm, sproj),
-        )
-    ):
-        loads.append(pltpu.make_async_copy(hbm, vmem, load_sem.at[index]))
-        loads[-1].start()
+    mates = ((1, sibling), (2, across), (3, corner))
+    level = {1: i + 1 - 2 * (i % 2), 2: (i + 2) % n_img, 3: n_img - 1 - i}
 
     barrier = pltpu.get_barrier_semaphore()
     for step in range(1, n_img * n_cap):
         peer = {"img": (i + step // n_cap) % n_img, "cap": (j + step % n_cap) % n_cap}
         pl.semaphore_signal(barrier, inc=1, device_id=peer, device_id_type=MESH)
 
-    def remote(source, target, kind, step, to_img, to_cap):
-        return pltpu.make_async_remote_copy(
-            src_ref=source,
-            dst_ref=target,
+    loads = {}
+    for index, (name, hbm, vmem) in enumerate(
+        (
+            ("text", text_hbm, text_ref),
+            ("feats", feats_hbm, feats_ref),
+            ("quarter", query_hbm.at[pl.ds(j * part_img, part_img)], quarter),
+            ("vproj", vproj_hbm, vproj),
+            ("tproj", tproj_hbm, tproj),
+            ("states", states_hbm, states),
+            ("query", query_hbm, query),
+            ("cand", cand_hbm, cand_ref),
+            ("lens", lens_hbm, lens_ref),
+            ("sproj", sproj_hbm, sproj),
+        )
+    ):
+        loads[name] = pltpu.make_async_copy(hbm, vmem, load_sem.at[index])
+        loads[name].start()
+
+    def remote(block, kind, step, to_img, to_cap):
+        copy = pltpu.make_async_remote_copy(
+            src_ref=block,
+            dst_ref=block,
             send_sem=send_sem.at[kind, step],
             recv_sem=recv_sem.at[kind, step],
             device_id={"img": to_img, "cap": to_cap},
             device_id_type=MESH,
         )
-
-    mine = packs.at[i, j]
+        copy.start()
+        return copy
+
+    mine, side = (packs.at[i, j], sides.at[i, j])
+    loads["text"].wait()
+    loads["feats"].wait()
     text = text_ref[...]
-    mine[pl.ds(text_at, 16), :] = text[:, :itc]
-    mine[pl.ds(text_at + 16, 16), :] = text[:, itc:]
+    side[pl.ds(0, 16), :] = text[:, :itc]
+    side[pl.ds(16, 16), :] = text[:, itc:]
     row = lax.broadcasted_iota(jnp.int32, (n_cap * 8, img_dev), 0)
     column = lax.broadcasted_iota(jnp.int32, (n_cap * 8, img_dev), 1)
     wanted = jnp.where(row % 8 < part_img, (row // 8) * part_img + row % 8, -1)
@@ -207,34 +223,28 @@
 
         @pl.when(j == part)
         def _():
-            mine[pl.ds(feat_at, 32), :] = placed[:, begin : begin + itc]
-
-    loads[0].wait()
-    loads[1].wait()
-    own_rows[...] = unit_rows(
-        jnp.dot(
-            query[...].reshape(img_dev * queries, width),
-            vproj[...],
-            preferred_element_type=jnp.float32,
-        )
-    ).astype(jnp.bfloat16)
-    mine[pl.ds(0, part_rows), :] = own_rows[
-        pl.ds(pl.multiple_of(j * part_rows, part_rows), part_rows), :
-    ]
+            side[pl.ds(32, 32), :] = placed[:, begin : begin + itc]
+
     pl.semaphore_wait(barrier, n_img * n_cap - 1)
-
-    along = {}
-    for step in NEAR_FIRST:
-        along[step] = remote(mine, mine, 0, step, (i + step) % n_img, j)
-        along[step].start()
-    texts = {}
-    for step, peer in ((1, sibling), (2, across), (3, corner)):
-        piece = mine.at[pl.ds(text_at, 32), :]
-        texts[step] = remote(piece, piece, 4, step, i, peer)
-        texts[step].start()
-
-    loads[2].wait()
-    loads[3].wait()
+    side_along = {step: remote(side, 0, step, level[step], j) for step in STEPS}
+    texts = {
+        step: remote(side.at[pl.ds(0, 32), :], 1, step, i, peer) for step, peer in mates
+    }
+
+    def rows_of(values):
+        return unit_rows(
+            jnp.dot(
+                values.reshape(-1, width), vproj[...], preferred_element_type=jnp.float32
+            )
+        ).astype(jnp.bfloat16)
+
+    loads["quarter"].wait()
+    loads["vproj"].wait()
+    mine[...] = rows_of(quarter[...])
+    along = {step: remote(mine, 2, step, level[step], j) for step in STEPS}
+
+    loads["states"].wait()
+    loads["tproj"].wait()
     tokens[...] = unit_rows(
         jnp.dot(
             states[...].reshape(cap_dev * length, width),
@@ -244,21 +254,50 @@
     ).astype(jnp.bfloat16)
     strong[...] = jnp.zeros_like(strong)
 
+    side_over, side_beside, side_onward = ({}, {}, {})
+    for step in STEPS:
+        side_along[step].wait_recv()
+        block = sides.at[level[step], j]
+        side_over[step] = remote(block, 3, step, i, across)
+        side_beside[step] = remote(block, 4, step, i, sibling)
+
     def score(rows, owner, part):
         products = lax.dot_general(rows, tokens[...], LAST, preferred_element_type=jnp.float32)
         strong[owner * n_cap + part, :part_img, :] = jnp.max(
             products.reshape(part_img, queries, cap_dev * length), axis=1
         )
 
+    loads["query"].wait()
+    own_rows[...] = rows_of(query[...])
     for part in range(n_cap):
         score(own_rows[pl.ds(part * part_rows, part_rows), :], i, part)
 
+    def use(owner, part):
+        score(packs[owner, part], owner, part)
+
+    over, beside, onward = ({}, {}, {})
+
+    def pass_on(step):
+        along[step].wait_recv()
+        block = packs.at[level[step], j]
+        over[step] = remote(block, 6, step, i, across)
+        beside[step] = remote(block, 7, step, i, sibling)
+        use(level[step], j)
+
+    pass_on(1)
+    for step in STEPS:
+        side_over[step].wait_recv()
+        side_onward[step] = remote(sides.at[level[step], across], 5, step, i, sibling)
+
+    loads["cand"].wait()
     slot = lax.broadcasted_iota(jnp.int32, (cap_dev, slots), 1)
     image = jnp.where(slot % 8 < part_img, (slot // 8) * part_img + slot % 8, -1)
     counts = jnp.zeros((cap_dev, slots), jnp.float32)
     cand = cand_ref[...]
     for k in range(cand.shape[1]):
         counts += (cand[:, k : k + 1] == image).astype(jnp.float32)
+    present = counts > 0
+    loads["lens"].wait()
     caption = lax.broadcasted_iota(jnp.int32, (cap_dev, 1), 0)
     lens = jnp.zeros((cap_dev, 1), jnp.int32)
     for c in range(cap_dev):
@@ -267,66 +306,64 @@
     at = place - caption * length
     mask = ((at >= 0) & (at < lens)).astype(jnp.bfloat16)
 
+    pass_on(2)
+
     def use_text(owner, part):
         begin = pl.multiple_of((owner * n_cap + part) * 16, 16)
-        text_all[pl.ds(begin, 16), :itc] = packs[owner, part, pl.ds(text_at, 16), :]
-        text_all[pl.ds(begin, 16), itc:] = packs[owner, part, pl.ds(text_at + 16, 16), :]
-
-    def use(owner, part):
-        score(packs[owner, part, pl.ds(0, part_rows), :], owner, part)
+        text_all[pl.ds(begin, 16), :itc] = sides[owner, part, pl.ds(0, 16), :]
+        text_all[pl.ds(begin, 16), itc:] = sides[owner, part, pl.ds(16, 16), :]
+
+    def use_side(owner, part):
         use_text(owner, part)
         rows = pl.ds(pl.multiple_of(owner * n_cap * 8, n_cap * 8), n_cap * 8)
         begin = pl.multiple_of(jnp.minimum(part, width // itc - 1) * itc, itc)
-        feats_all[rows, pl.ds(begin, itc)] = packs[owner, part, pl.ds(feat_at, 32), :]
-
-    over, beside, onward = ({}, {}, {})
-    for step in NEAR_FIRST:
-        owner = (i - step + n_img) % n_img
-        along[step].wait_recv()
-        block = packs.at[owner, j]
-        over[step] = remote(block, block, 1, step, i, across)
-        over[step].start()
-        beside[step] = remote(block, block, 2, step, i, sibling)
-        beside[step].start()
-        use(owner, j)
+        feats_all[rows, pl.ds(begin, itc)] = sides[owner, part, pl.ds(32, 32), :]
+
     use_text(i, j)
-    for step, peer in ((1, sibling), (2, across), (3, corner)):
+    for step, peer in mates:
         texts[step].wait_recv()
         use_text(i, peer)
-    for step in NEAR_FIRST:
-        owner = (i - step + n_img) % n_img
-        over[step].wait_recv()
-        block = packs.at[owner, across]
-        onward[step] = remote(block, block, 3, step, i, sibling)
-        onward[step].start()
-        use(owner, across)
-        beside[step].wait_recv()
-        use(owner, sibling)
-    for step in NEAR_FIRST:
-        onward[step].wait_recv()
-        use((i - step + n_img) % n_img, corner)
-
-    loads[4].wait()
+    for step in STEPS:
+        use_side(level[step], j)
+        use_side(level[step], across)
+        side_beside[step].wait_recv()
+        use_side(level[step], sibling)
+        side_onward[step].wait_recv()
+        use_side(level[step], corner)
+
+    def log_softmax(scores):
+        peak = jnp.max(jnp.where(present, scores, -jnp.inf), axis=1, keepdims=True)
+        shifted = jnp.where(present, scores - peak, 0.0)
+        total = jnp.sum(counts * jnp.exp(shifted), axis=1, keepdims=True)
+        return shifted - jnp.log(total)
+
+    loads["sproj"].wait()
     embed = jnp.dot(feats_all[...], sproj[...], preferred_element_type=jnp.float32)
     norm = jnp.sqrt(jnp.sum(embed * embed, axis=-1, keepdims=True) + 1e-06)
     unit = embed / norm
     wide = text.astype(jnp.float32)
     text_scale = lax.rsqrt(jnp.sum(wide * wide, axis=-1, keepdims=True) + 1e-06)
-    student = LOGIT_SCALE * (product_three(text, unit) * text_scale)
+    student_log = log_softmax(LOGIT_SCALE * (product_three(text, unit) * text_scale))
+    student_prob = jnp.exp(student_log)
+    turned = feats_all[...].astype(jnp.float32).T.astype(jnp.bfloat16)
+    feats_out_ref[:, :slots] = turned
+    feats_out_ref[:, slots:] = turned
+
+    pass_on(3)
+    for step in STEPS:
+        over[step].wait_recv()
+        onward[step] = remote(packs.at[level[step], across], 8, step, i, sibling)
+        beside[step].wait_recv()
+        use(level[step], sibling)
+        use(level[step], across)
+    for step in STEPS:
+        onward[step].wait_recv()
+        use(level[step], corner)
+
     summed = product_three(mask, strong[...].reshape(slots, cap_dev * length))
-    teacher = summed / lens.astype(jnp.float32) / TEACHER_TEMP
-    present = counts > 0
-
-    def log_softmax(scores):
-        peak = jnp.max(jnp.where(present, scores, -jnp.inf), axis=1, keepdims=True)
-        shifted = jnp.where(present, scores - peak, 0.0)
-        total = jnp.sum(counts * jnp.exp(shifted), axis=1, keepdims=True)
-        return shifted - jnp.log(total)
-
-    teacher_log = log_softmax(teacher)
-    student_log = log_softmax(student)
+    teacher_log = log_softmax(summed / lens.astype(jnp.float32) / TEACHER_TEMP)
     teacher_prob = jnp.exp(teacher_log)
-    spreads[i, j] = (LOGIT_SCALE * text_scale) * (counts * (jnp.exp(student_log) - teacher_prob))
+    spreads[i, j] = (LOGIT_SCALE * text_scale) * (counts * (student_prob - teacher_prob))
     sent = []
     for step in range(1, n_img * n_cap):
         sent.append(
@@ -343,14 +380,12 @@
             )
         )
         sent[-1].start()
-    losses_ref[...] = jnp.sum(
-        counts * teacher_prob * (teacher_log - student_log), axis=1, keepdims=True
-    )
-    turned = feats_all[...].astype(jnp.float32).T.astype(jnp.bfloat16)
-    feats_out_ref[:, :slots] = turned
-    feats_out_ref[:, slots:] = turned
-    for copies in (along, over, beside, onward, texts):
-        for step in NEAR_FIRST:
+    terms = counts * teacher_prob * (teacher_log - student_log)
+    losses_ref[...] = jnp.sum(terms.T, axis=0, keepdims=True)
+    for copies in (
+        side_along, side_over, side_beside, side_onward, along, over, beside, onward, texts
+    ):
+        for step in STEPS:
             copies[step].wait_send()
     for copy in sent:
         copy.wait_recv()
@@ -384,51 +419,51 @@
     itc = text_proj.shape[1]
     embed_width = student_proj.shape[1]
     slots = n_img * n_cap * 8
-    part_rows = img_dev * queries // n_cap
+    part_img = img_dev // n_cap
     vmem = pl.BlockSpec(memory_space=pltpu.VMEM)
-    anywhere = pl.BlockSpec(memory_space=pl.ANY)
+    args = (
+        text_states,
+        text_lens,
+        text_proj,
+        query_states,
+        vision_proj,
+        student_text,
+        student_feats,
+        student_proj,
+        candidates,
+    )
+    held = [pltpu.VMEM(arg.shape, arg.dtype) for arg in args]
+    held[1] = pltpu.SMEM(text_lens.shape, text_lens.dtype)
     losses, grads, feats = pl.pallas_call(
         fused_kernel,
         out_shape=(
-            jax.ShapeDtypeStruct((cap_dev, 1), jnp.float32),
+            jax.ShapeDtypeStruct((1, cap_dev), jnp.float32),
             jax.ShapeDtypeStruct((2 * slots, embed_width), jnp.bfloat16),
             jax.ShapeDtypeStruct((width, 2 * slots), jnp.bfloat16),
         ),
-        in_specs=[pl.BlockSpec(memory_space=pltpu.SMEM)] + [vmem] * 3 + [anywhere] * 5,
+        in_specs=[pl.BlockSpec(memory_space=pltpu.HBM)] * len(args),
         out_specs=(vmem, vmem, vmem),
-        scratch_shapes=[
-            pltpu.VMEM(text_states.shape, jnp.bfloat16),
-            pltpu.VMEM(text_proj.shape, jnp.bfloat16),
-            pltpu.VMEM(query_states.shape, jnp.bfloat16),
-            pltpu.VMEM(vision_proj.shape, jnp.bfloat16),
-            pltpu.VMEM(student_proj.shape, jnp.bfloat16),
-            pltpu.VMEM((n_img, n_cap, part_rows + 64, itc), jnp.bfloat16),
+        scratch_shapes=held
+        + [
+            pltpu.VMEM((part_img, queries, width), jnp.bfloat16),
+            pltpu.VMEM((n_img, n_cap, part_img * queries, itc), jnp.bfloat16),
+            pltpu.VMEM((n_img, n_cap, 64, itc), jnp.bfloat16),
             pltpu.VMEM((img_dev * queries, itc), jnp.bfloat16),
             pltpu.VMEM((cap_dev * length, itc), jnp.bfloat16),
             pltpu.VMEM((n_img * n_cap, 8, cap_dev * length), jnp.float32),
             pltpu.VMEM((n_img, n_cap, cap_dev, slots), jnp.float32),
             pltpu.VMEM((slots, width), jnp.bfloat16),
             pltpu.VMEM((n_img * n_cap * cap_dev, embed_width), jnp.bfloat16),
-            pltpu.SemaphoreType.DMA((5,)),
-            pltpu.SemaphoreType.DMA((5, 4)),
-            pltpu.SemaphoreType.DMA((5, 4)),
+            pltpu.SemaphoreType.DMA((10,)),
+            pltpu.SemaphoreType.DMA((9, 4)),
+            pltpu.SemaphoreType.DMA((9, 4)),
             pltpu.SemaphoreType.DMA((n_img * n_cap,)),
             pltpu.SemaphoreType.DMA((n_img * n_cap,)),
         ],
         compiler_params=pltpu.CompilerParams(
-            collective_id=0, has_side_effects=True, vmem_limit_bytes=48 * 1024 * 1024
+            collective_id=0, has_side_effects=True, vmem_limit_bytes=60 * 1024 * 1024
         ),
-    )(
-        text_lens,
-        candidates,
-        student_text,
-        student_feats,
-        text_states,
-        text_proj,
-        query_states,
-        vision_proj,
-        student_proj,
-    )
+    )(*args)
     proj_grad = jnp.dot(feats, grads, preferred_element_type=jnp.float32)
     return (losses.reshape(cap_dev), proj_grad)
 

time: 44.2 us -> 35.8 us (0.81)
  local copies, waits for them, and re-layouts: 8.35 us -> 0.52 us
  matrix products: 1.5 us -> 2.57 us
  Pallas kernels: 32.6 us -> 31.9 us
  other arithmetic: 0.63 us -> 0 us
    unnamed x18 -> x3, local copies, waits for them, and re-layouts: 8.35 us -> 0.52 us
    dot_general x1, matrix products: 1.5 us -> 2.57 us  [fused(): proj_grad = jnp.dot(feats, grads, preferred_element_type=jnp.float32)]
    pallas_call x1, Pallas kernels: 32.6 us -> 31.9 us  [fused(): pl.pallas_call(fused_kernel, out_shape=(jax.ShapeDtypeStruct((1, cap_dev)...]
    pallas_call x1 -> x0, other arithmetic: 0.63 us -> none  [fused(): pl.pallas_call(fused_kernel, out_shape=(jax.ShapeDtypeStruct((cap_dev, 1)...]
where the time goes in v3:
time: 35.8 us; the launch traced here: 35.6 us
  Pallas kernels  31.9 us (89%)
  matrix products  2.57 us (7%)
  between operations  0.65 us (2%)
  local copies, waits for them, and re-layouts  0.52 us (1%)
    pallas_call x1, Pallas kernels, fused(): pl.pallas_call(fused_kernel, out_shape=(jax.ShapeDtypeStruct((1, cap_dev)...  31.9 us
    dot_general x1, matrix products, fused(): proj_grad = jnp.dot(feats, grads, preferred_element_type=jnp.float32)  2.57 us

profile of v3, /device:TPU:0, one launch (start us, length us, event | category | flops | bytes accessed | tf_op | source)
XLA Modules:
  0.0 35.6 jit_solution(4075772993929855419)
XLA Ops:
  0.6 31.9 %shard_map.104 = (f32[1,16]{1,0:T(1,128)}, bf16[256,512]{1,0:T(8,128)(2,1)}, bf16[768,256]{1,0:T(8,128)(2,1)}) custom-call(bf16[16,32,768]{2,1,0:T(8,128)(2,1)} %states_hbm.1, s32[16]{0:T(128)} %lens_hbm.1, bf16[768,256]{1,0:T(8,128)(2,1)} %tproj_hbm.1, bf16[24,32,768]{2,1,0:T(8,128)(2,1)} %query_hbm.1, bf16[768,256]{1,0:T(8,128)(2,1)} %vproj_hbm.1, ...), custom_call_target="tpu_custom_call" | custom-call | tf_op jit(solution)/shard_map/pallas_call | solution.py:437
  32.5 0.0 copy-start
  32.5 2.6 %fusion = f32[768,512]{1,0:T(8,128)} fusion(bf16[768,256]{1,0:T(8,128)(2,1)} %get-tuple-element.6, bf16[256,512]{1,0:T(8,128)(2,1)} %get-tuple-element.7), kind=kOutput, calls=%fused_computation | convolution fusion | flops 201326592 | bytes 2228224 | tf_op jit(solution)/shard_map/dot_general | solution.py:467
  35.1 0.0 copy-done
  35.1 0.5 %copy.12 = f32[16]{0:T(128)} copy(f32[16]{0:T(128)S(1)} %bitcast.3) | data formatting | bytes 128
Async XLA Ops:
  32.5 2.6 %copy-start = (f32[1,16]{1,0:T(1,128)S(1)}, f32[1,16]{1,0:T(1,128)}, u32[]{:S(2)}) copy-start(f32[1,16]{1,0:T(1,128)} %get-tuple-element.5) | copy-start | bytes 196

commit v4 on v3

--- a/solution.py
+++ b/solution.py
@@ -100,6 +100,7 @@
 MESH = pl.DeviceIdType.MESH
 LAST = (((1,), (1,)), ((), ()))
 STEPS = (1, 2, 3)
+CHUNKS = 1
 
 
 def split_three(values):
@@ -141,7 +142,7 @@
     cand_ref,
     quarter,
     packs,
-    sides,
+    side_parts,
     own_rows,
     tokens,
     strong,
@@ -166,13 +167,14 @@
     sibling = 2 * chip + (1 - core)
     across = 2 * (1 - chip) + core
     corner = 2 * (1 - chip) + (1 - core)
-    mates = ((1, sibling), (2, across), (3, corner))
-    level = {1: i + 1 - 2 * (i % 2), 2: (i + 2) % n_img, 3: n_img - 1 - i}
+    mates = ((1, sibling), (2, across))
+    level = {0: i, 1: i + 1 - 2 * (i % 2), 2: (i + 2) % n_img, 3: n_img - 1 - i}
 
     barrier = pltpu.get_barrier_semaphore()
-    for step in range(1, n_img * n_cap):
-        peer = {"img": (i + step // n_cap) % n_img, "cap": (j + step % n_cap) % n_cap}
-        pl.semaphore_signal(barrier, inc=1, device_id=peer, device_id_type=MESH)
+    for to_img, to_cap in ((level[1], j), (level[2], j), (i, sibling), (i, across)):
+        pl.semaphore_signal(
+            barrier, inc=1, device_id={"img": to_img, "cap": to_cap}, device_id_type=MESH
+        )
 
     loads = {}
     for index, (name, hbm, vmem) in enumerate(
@@ -192,24 +194,62 @@
         loads[name] = pltpu.make_async_copy(hbm, vmem, load_sem.at[index])
         loads[name].start()
 
-    def remote(block, kind, step, to_img, to_cap):
+    def remote(block, stream, kind, step, to_img, to_cap):
         copy = pltpu.make_async_remote_copy(
             src_ref=block,
             dst_ref=block,
-            send_sem=send_sem.at[kind, step],
-            recv_sem=recv_sem.at[kind, step],
+            send_sem=send_sem.at[stream, kind, step],
+            recv_sem=recv_sem.at[stream, kind, step],
             device_id={"img": to_img, "cap": to_cap},
             device_id_type=MESH,
         )
         copy.start()
         return copy
 
-    mine, side = (packs.at[i, j], sides.at[i, j])
+    class Stream:
+        def __init__(self, index, block):
+            self.index, self.block = (index, block)
+            self.along, self.over, self.beside, self.onward = ({}, {}, {}, {})
+
+        def start(self):
+            for step in (2, 1):
+                self.along[step] = remote(self.block(i, j), self.index, 0, step, level[step], j)
+
+        def pass_on(self, step):
+            self.along[step].wait_recv()
+            block = self.block(level[step], j)
+            if step == 2:
+                self.along[3] = remote(block, self.index, 0, 3, level[1], j)
+            self.over[step] = remote(block, self.index, 1, step, i, across)
+            self.beside[step] = remote(block, self.index, 2, step, i, sibling)
+
+        def turn(self, step):
+            self.over[step].wait_recv()
+            self.onward[step] = remote(
+                self.block(level[step], across), self.index, 3, step, i, sibling
+            )
+
+        def sent(self):
+            for copies in (self.along, self.over, self.beside, self.onward):
+                for step in STEPS:
+                    copies[step].wait_send()
+
+    chunk_img = part_img // CHUNKS
+    chunk_rows = chunk_img * queries
+    side_stream = Stream(0, lambda owner, part: side_parts.at[owner, part])
+
+    def chunk_of(chunk):
+        return lambda owner, part: packs.at[
+            owner, part, pl.ds(chunk * chunk_rows, chunk_rows), :
+        ]
+
+    row_streams = [Stream(1 + chunk, chunk_of(chunk)) for chunk in range(CHUNKS)]
+
     loads["text"].wait()
     loads["feats"].wait()
     text = text_ref[...]
-    side[pl.ds(0, 16), :] = text[:, :itc]
-    side[pl.ds(16, 16), :] = text[:, itc:]
+    side_parts[i, j, 32:48, :] = text[:, :itc]
+    side_parts[i, j, 48:, :] = text[:, itc:]
     row = lax.broadcasted_iota(jnp.int32, (n_cap * 8, img_dev), 0)
     column = lax.broadcasted_iota(jnp.int32, (n_cap * 8, img_dev), 1)
     wanted = jnp.where(row % 8 < part_img, (row // 8) * part_img + row % 8, -1)
@@ -223,13 +263,16 @@
 
         @pl.when(j == part)
         def _():
-            side[pl.ds(32, 32), :] = placed[:, begin : begin + itc]
-
-    pl.semaphore_wait(barrier, n_img * n_cap - 1)
-    side_along = {step: remote(side, 0, step, level[step], j) for step in STEPS}
-    texts = {
-        step: remote(side.at[pl.ds(0, 32), :], 1, step, i, peer) for step, peer in mates
-    }
+            side_parts[i, j, :32, :] = placed[:, begin : begin + itc]
+
+    pl.semaphore_wait(barrier, 4)
+    side_stream.start()
+
+    def own_text(part, step, to_cap):
+        block = side_parts.at[i, part, pl.ds(32, 32), :]
+        return remote(block, 1 + CHUNKS, 0, step, i, to_cap)
+
+    texts = {step: own_text(j, step, peer) for step, peer in mates}
 
     def rows_of(values):
         return unit_rows(
@@ -240,9 +283,11 @@
 
     loads["quarter"].wait()
     loads["vproj"].wait()
-    mine[...] = rows_of(quarter[...])
-    along = {step: remote(mine, 2, step, level[step], j) for step in STEPS}
-
+    for chunk in range(CHUNKS):
+        packs[i, j, pl.ds(chunk * chunk_rows, chunk_rows), :] = rows_of(
+            quarter[pl.ds(chunk * chunk_img, chunk_img)]
+        )
+        row_streams[chunk].start()
     loads["states"].wait()
     loads["tproj"].wait()
     tokens[...] = unit_rows(
@@ -254,41 +299,52 @@
     ).astype(jnp.bfloat16)
     strong[...] = jnp.zeros_like(strong)
 
-    side_over, side_beside, side_onward = ({}, {}, {})
-    for step in STEPS:
-        side_along[step].wait_recv()
-        block = sides.at[level[step], j]
-        side_over[step] = remote(block, 3, step, i, across)
-        side_beside[step] = remote(block, 4, step, i, sibling)
-
-    def score(rows, owner, part):
+    def score(rows, owner, part, at, count):
         products = lax.dot_general(rows, tokens[...], LAST, preferred_element_type=jnp.float32)
-        strong[owner * n_cap + part, :part_img, :] = jnp.max(
-            products.reshape(part_img, queries, cap_dev * length), axis=1
-        )
-
+        strong[owner * n_cap + part, at : at + count, :] = jnp.max(
+            products.reshape(count, queries, cap_dev * length), axis=1
+        )
+
+    def use(owner, part, chunk):
+        score(chunk_of(chunk)(owner, part)[...], owner, part, chunk * chunk_img, chunk_img)
+
+    def use_text(owner, part):
+        begin = pl.multiple_of((owner * n_cap + part) * 16, 16)
+        text_all[pl.ds(begin, 16), :itc] = side_parts[owner, part, 32:48, :]
+        text_all[pl.ds(begin, 16), itc:] = side_parts[owner, part, 48:, :]
+
+    def use_feats(owner, part):
+        rows = pl.ds(pl.multiple_of(owner * n_cap * 8, n_cap * 8), n_cap * 8)
+        begin = pl.multiple_of(jnp.minimum(part, width // itc - 1) * itc, itc)
+        feats_all[rows, pl.ds(begin, itc)] = side_parts[owner, part, :32, :]
+
+    def log_softmax(scores):
+        peak = jnp.max(jnp.where(present, scores, -jnp.inf), axis=1, keepdims=True)
+        shifted = jnp.where(present, scores - peak, 0.0)
+        total = jnp.sum(counts * jnp.exp(shifted), axis=1, keepdims=True)
+        return shifted - jnp.log(total)
+
+    def forward(step):
+        for chunk in range(CHUNKS):
+            row_streams[chunk].pass_on(step)
+
+    def score_block(owner, part):
+        for chunk in range(CHUNKS):
+            use(owner, part, chunk)
+
+    side_stream.pass_on(1)
+    side_stream.pass_on(2)
+    forward(1)
+    forward(2)
     loads["query"].wait()
     own_rows[...] = rows_of(query[...])
     for part in range(n_cap):
-        score(own_rows[pl.ds(part * part_rows, part_rows), :], i, part)
-
-    def use(owner, part):
-        score(packs[owner, part], owner, part)
-
-    over, beside, onward = ({}, {}, {})
-
-    def pass_on(step):
-        along[step].wait_recv()
-        block = packs.at[level[step], j]
-        over[step] = remote(block, 6, step, i, across)
-        beside[step] = remote(block, 7, step, i, sibling)
-        use(level[step], j)
-
-    pass_on(1)
-    for step in STEPS:
-        side_over[step].wait_recv()
-        side_onward[step] = remote(sides.at[level[step], across], 5, step, i, sibling)
-
+        score(own_rows[pl.ds(part * part_rows, part_rows), :], i, part, 0, part_img)
+    score_block(level[1], j)
+    side_stream.pass_on(3)
+    forward(3)
+    score_block(level[2], j)
+    score_block(level[3], j)
     loads["cand"].wait()
     slot = lax.broadcasted_iota(jnp.int32, (cap_dev, slots), 1)
     image = jnp.where(slot % 8 < part_img, (slot // 8) * part_img + slot % 8, -1)
@@ -305,38 +361,29 @@
     place = lax.broadcasted_iota(jnp.int32, (cap_dev, cap_dev * length), 1)
     at = place - caption * length
     mask = ((at >= 0) & (at < lens)).astype(jnp.bfloat16)
-
-    pass_on(2)
-
-    def use_text(owner, part):
-        begin = pl.multiple_of((owner * n_cap + part) * 16, 16)
-        text_all[pl.ds(begin, 16), :itc] = sides[owner, part, pl.ds(0, 16), :]
-        text_all[pl.ds(begin, 16), itc:] = sides[owner, part, pl.ds(16, 16), :]
-
-    def use_side(owner, part):
-        use_text(owner, part)
-        rows = pl.ds(pl.multiple_of(owner * n_cap * 8, n_cap * 8), n_cap * 8)
-        begin = pl.multiple_of(jnp.minimum(part, width // itc - 1) * itc, itc)
-        feats_all[rows, pl.ds(begin, itc)] = sides[owner, part, pl.ds(32, 32), :]
-
-    use_text(i, j)
-    for step, peer in mates:
-        texts[step].wait_recv()
-        use_text(i, peer)
     for step in STEPS:
-        use_side(level[step], j)
-        use_side(level[step], across)
-        side_beside[step].wait_recv()
-        use_side(level[step], sibling)
-        side_onward[step].wait_recv()
-        use_side(level[step], corner)
-
-    def log_softmax(scores):
-        peak = jnp.max(jnp.where(present, scores, -jnp.inf), axis=1, keepdims=True)
-        shifted = jnp.where(present, scores - peak, 0.0)
-        total = jnp.sum(counts * jnp.exp(shifted), axis=1, keepdims=True)
-        return shifted - jnp.log(total)
-
+        for chunk in range(CHUNKS):
+            row_streams[chunk].turn(step)
+        side_stream.turn(step)
+        if step == 1:
+            texts[2].wait_recv()
+            texts[3] = own_text(across, 3, sibling)
+        if step < 3:
+            for chunk in range(CHUNKS):
+                row_streams[chunk].beside[step].wait_recv()
+                use(level[step], sibling, chunk)
+                use(level[step], across, chunk)
+    score_block(level[3], across)
+    for chunk in range(CHUNKS):
+        row_streams[chunk].beside[3].wait_recv()
+        use(level[3], sibling, chunk)
+    for step in STEPS:
+        use_feats(level[step], j)
+        use_feats(level[step], across)
+        side_stream.beside[step].wait_recv()
+        use_feats(level[step], sibling)
+        side_stream.onward[step].wait_recv()
+        use_feats(level[step], corner)
     loads["sproj"].wait()
     embed = jnp.dot(feats_all[...], sproj[...], preferred_element_type=jnp.float32)
     norm = jnp.sqrt(jnp.sum(embed * embed, axis=-1, keepdims=True) + 1e-06)
@@ -348,46 +395,62 @@
     turned = feats_all[...].astype(jnp.float32).T.astype(jnp.bfloat16)
     feats_out_ref[:, :slots] = turned
     feats_out_ref[:, slots:] = turned
-
-    pass_on(3)
     for step in STEPS:
-        over[step].wait_recv()
-        onward[step] = remote(packs.at[level[step], across], 8, step, i, sibling)
-        beside[step].wait_recv()
-        use(level[step], sibling)
-        use(level[step], across)
-    for step in STEPS:
-        onward[step].wait_recv()
-        use(level[step], corner)
+        for chunk in range(CHUNKS):
+            row_streams[chunk].onward[step].wait_recv()
+            use(level[step], corner, chunk)
 
     summed = product_three(mask, strong[...].reshape(slots, cap_dev * length))
     teacher_log = log_softmax(summed / lens.astype(jnp.float32) / TEACHER_TEMP)
     teacher_prob = jnp.exp(teacher_log)
     spreads[i, j] = (LOGIT_SCALE * text_scale) * (counts * (student_prob - teacher_prob))
-    sent = []
-    for step in range(1, n_img * n_cap):
-        sent.append(
-            pltpu.make_async_remote_copy(
-                src_ref=spreads.at[i, j],
-                dst_ref=spreads.at[i, j],
-                send_sem=spread_send.at[step],
-                recv_sem=spread_recv.at[step],
-                device_id={
-                    "img": (i + step // n_cap) % n_img,
-                    "cap": (j + step % n_cap) % n_cap,
-                },
-                device_id_type=MESH,
-            )
-        )
-        sent[-1].start()
+    def spread_copy(block, index, to_img, to_cap):
+        copy = pltpu.make_async_remote_copy(
+            src_ref=block,
+            dst_ref=block,
+            send_sem=spread_send.at[index],
+            recv_sem=spread_recv.at[index],
+            device_id={"img": to_img, "cap": to_cap},
+            device_id_type=MESH,
+        )
+        copy.start()
+        return copy
+
+    direct = {
+        2 * step + side: spread_copy(
+            spreads.at[i, j], 2 * step + side, level[step], across if side else j
+        )
+        for step, side in ((3, 1), (3, 0), (2, 1), (2, 0), (1, 1), (1, 0), (0, 1))
+    }
+    relayed = [spread_copy(spreads.at[i, j], 8, i, sibling)]
     terms = counts * teacher_prob * (teacher_log - student_log)
     losses_ref[...] = jnp.sum(terms.T, axis=0, keepdims=True)
-    for copies in (
-        side_along, side_over, side_beside, side_onward, along, over, beside, onward, texts
-    ):
-        for step in STEPS:
-            copies[step].wait_send()
-    for copy in sent:
+    use_text(i, j)
+    use_text(i, across)
+    texts[1].wait_recv()
+    use_text(i, sibling)
+    texts[3].wait_recv()
+    use_text(i, corner)
+    for step in STEPS:
+        use_text(level[step], j)
+        use_text(level[step], across)
+        use_text(level[step], sibling)
+        use_text(level[step], corner)
+    for step, side in ((0, 1), (1, 0), (1, 1), (2, 0), (2, 1), (3, 0), (3, 1)):
+        direct[2 * step + side].wait_recv()
+        relayed.append(
+            spread_copy(
+                spreads.at[level[step], across if side else j],
+                8 + 2 * step + side,
+                i,
+                sibling,
+            )
+        )
+    for stream in [side_stream] + row_streams:
+        stream.sent()
+    for step in STEPS:
+        texts[step].wait_send()
+    for copy in relayed:
         copy.wait_recv()
     across_captions = spreads[...].reshape(n_img * n_cap * cap_dev, slots).T
     total = jnp.zeros(embed.shape, jnp.float32)
@@ -398,7 +461,7 @@
     top = embed_grad.astype(jnp.bfloat16)
     grad_ref[:slots, :] = top
     grad_ref[slots:, :] = (embed_grad - top.astype(jnp.float32)).astype(jnp.bfloat16)
-    for copy in sent:
+    for copy in list(direct.values()) + relayed:
         copy.wait_send()
 
 
@@ -455,8 +518,8 @@
             pltpu.VMEM((slots, width), jnp.bfloat16),
             pltpu.VMEM((n_img * n_cap * cap_dev, embed_width), jnp.bfloat16),
             pltpu.SemaphoreType.DMA((10,)),
-            pltpu.SemaphoreType.DMA((9, 4)),
-            pltpu.SemaphoreType.DMA((9, 4)),
+            pltpu.SemaphoreType.DMA((2 + CHUNKS, 4, 4)),
+            pltpu.SemaphoreType.DMA((2 + CHUNKS, 4, 4)),
             pltpu.SemaphoreType.DMA((n_img * n_cap,)),
             pltpu.SemaphoreType.DMA((n_img * n_cap,)),
         ],

time: 35.8 us -> 34.3 us (0.958)
  Pallas kernels: 31.9 us -> 30.3 us
    pallas_call x1, Pallas kernels: 31.9 us -> 30.3 us  [fused(): pl.pallas_call(fused_kernel, out_shape=(jax.ShapeDtypeStruct((1, cap_dev)...]
where the time goes in v4:
time: 34.3 us; the launch traced here: 34.1 us
  Pallas kernels  30.3 us (88%)
  matrix products  2.58 us (8%)
  between operations  0.65 us (2%)
  local copies, waits for them, and re-layouts  0.52 us (2%)
    pallas_call x1, Pallas kernels, fused(): pl.pallas_call(fused_kernel, out_shape=(jax.ShapeDtypeStruct((1, cap_dev)...  30.3 us
    dot_general x1, matrix products, fused(): proj_grad = jnp.dot(feats, grads, preferred_element_type=jnp.float32)  2.58 us

profile of v4, /device:TPU:0, one launch (start us, length us, event | category | flops | bytes accessed | tf_op | source)
XLA Modules:
  0.0 34.1 jit_solution(4396912860386263236)
XLA Ops:
  0.6 30.3 %shard_map.104 = (f32[1,16]{1,0:T(1,128)}, bf16[256,512]{1,0:T(8,128)(2,1)}, bf16[768,256]{1,0:T(8,128)(2,1)}) custom-call(bf16[16,32,768]{2,1,0:T(8,128)(2,1)} %states_hbm.1, s32[16]{0:T(128)} %lens_hbm.1, bf16[768,256]{1,0:T(8,128)(2,1)} %tproj_hbm.1, bf16[24,32,768]{2,1,0:T(8,128)(2,1)} %query_hbm.1, bf16[768,256]{1,0:T(8,128)(2,1)} %vproj_hbm.1, ...), custom_call_target="tpu_custom_call" | custom-call | tf_op jit(solution)/shard_map/pallas_call | solution.py:500
  31.0 0.0 copy-start
  31.0 2.6 %fusion = f32[768,512]{1,0:T(8,128)} fusion(bf16[768,256]{1,0:T(8,128)(2,1)} %get-tuple-element.6, bf16[256,512]{1,0:T(8,128)(2,1)} %get-tuple-element.7), kind=kOutput, calls=%fused_computation | convolution fusion | flops 201326592 | bytes 2228224 | tf_op jit(solution)/shard_map/dot_general | solution.py:530
  33.5 0.0 copy-done
  33.5 0.5 %copy.12 = f32[16]{0:T(128)} copy(f32[16]{0:T(128)S(1)} %bitcast.3) | data formatting | bytes 128
Async XLA Ops:
  31.0 2.6 %copy-start = (f32[1,16]{1,0:T(1,128)S(1)}, f32[1,16]{1,0:T(1,128)}, u32[]{:S(2)}) copy-start(f32[1,16]{1,0:T(1,128)} %get-tuple-element.5) | copy-start | bytes 196
